TPU v7x, 32 devices: a whole 2x2x4 slice. The times are simulated.
32 devices in a mesh: seq: 2 (over y), fsdp: 16 (over z, x, core).
Axes of the slice: x: 2, y: 2, z: 4, core: 2. Of those that a mesh axis runs over, the one named last changes fastest.
Arguments:
- hidden: bfloat16 [16, 1024, 768], P('fsdp', 'seq'), may hold values from -6 to 6
- query_in: bfloat16 [16, 256, 768], P('fsdp', 'seq'), may hold values from -6 to 6
- memory: bfloat16 [16, 384, 768], P('fsdp', 'seq'), may hold values from -6 to 6
- segment_ids: int32 [16, 1408], P('fsdp'), may hold values from 0 to 2, never falling along the last dimension, each value on 1 to 704 neighbouring positions
- block_order: int32 [16, 4], P('fsdp'), may hold values from 0 to 3, each once within a row
- memory_valid: int32 [16, 384], P('fsdp'), may hold values 0 or 1
- w_query: bfloat16 [768, 768], P('fsdp'), may hold values from -0.21875 to 0.21875
- w_key: bfloat16 [768, 768], P('fsdp'), may hold values from -0.21875 to 0.21875
- w_value: bfloat16 [768, 768], P('fsdp'), may hold values from -0.21875 to 0.21875
- w_out: bfloat16 [768, 768], P('fsdp'), may hold values from -1.75 to 1.75
- w_rel: bfloat16 [768, 768], P('fsdp', 'seq'), may hold values from -0.21875 to 0.21875
- rel_biases: bfloat16 [3, 768], P(None, ('seq', 'fsdp')), may hold values from -3 to 3
- seg_embed: bfloat16 [2, 768], P(None, ('seq', 'fsdp')), may hold values from -3 to 3
- w_inner: bfloat16 [768, 3072], P('fsdp'), may hold values from -0.21875 to 0.21875
- b_inner: bfloat16 [3072], P('fsdp'), may hold values from -3 to 3
- w_outer: bfloat16 [3072, 768], P('fsdp'), may hold values from -0.109375 to 0.109375
- b_outer: bfloat16 [768], P('fsdp'), may hold values from -2 to 2
- norm_gains: bfloat16 [2, 768], P(None, 'fsdp'), may hold values from 0.5 to 1.5
- norm_biases: bfloat16 [2, 768], P(None, 'fsdp'), may hold values from -2 to 2
- grad_hidden_out: bfloat16 [16, 1024, 768], P('fsdp', 'seq'), may hold values from -6 to 6
- grad_query_out: bfloat16 [16, 256, 768], P('fsdp', 'seq'), may hold values from -6 to 6
Outputs:
- hidden_out: bfloat16 [16, 1024, 768], P('fsdp', 'seq')
- query_out: bfloat16 [16, 256, 768], P('fsdp', 'seq')
- grad_hidden: float32 [16, 1024, 768], P('fsdp', 'seq')
- grad_query: float32 [16, 256, 768], P('fsdp', 'seq')
- grad_w_query: float32 [768, 768], P(('seq', 'fsdp'))
- grad_w_key: float32 [768, 768], P(('seq', 'fsdp'))
- grad_w_value: float32 [768, 768], P(('seq', 'fsdp'))
- grad_w_out: float32 [768, 768], P(('seq', 'fsdp'))
- grad_w_rel: float32 [768, 768], P('fsdp', 'seq')
- grad_rel_biases: float32 [3, 768], P(None, ('seq', 'fsdp'))
- grad_seg_embed: float32 [2, 768], P(None, ('seq', 'fsdp'))
- grad_w_inner: float32 [768, 3072], P(('seq', 'fsdp'))
- grad_b_inner: float32 [3072], P(('seq', 'fsdp'))
- grad_w_outer: float32 [3072, 768], P(('seq', 'fsdp'))
- grad_b_outer: float32 [768], P(('seq', 'fsdp'))
- grad_norm_gains: float32 [2, 768], P(None, ('seq', 'fsdp'))
- grad_norm_biases: float32 [2, 768], P(None, ('seq', 'fsdp'))
Inputs may be any that keep to these rules, and one draw needn't show every extreme that they name: `segment_ids`: each row holds the segments of 384 memory slots, then of 1024 tokens, never falling. `block_order`: each row names each of the 4 blocks once.
All inputs are finite; a program needn't handle non-finite values. No bound on the sum of `memory_valid` on one device may be relied on, other than what follows from the above.
Results may differ from a plain program's by a relative error of at most 0.017.
Values may be sent and summed in bfloat16 or wider, within the bound.
No kernel may reach another device: no remote copies, remote signals or barrier semaphores. Data moves between devices by JAX's collectives and lax.ppermute only.
A program may use at most 256 MiB of HBM per device.

v0:
```python
import jax
import jax.numpy as jnp
from jax import lax
from jax.sharding import PartitionSpec as P

DH = 64
BLOCK = 256
NBLK = 4
MEM = 384
L = 1024


EPSILON = 1e-05
NEGATIVE = -1e30
SCORE_SCALE = 0.125
HIGHEST = lax.Precision.HIGHEST


def product(left, right):
    return jnp.dot(left, right, preferred_element_type=jnp.float32)


def inner_rows(left, right):
    return lax.dot_general(
        left, right, (((1,), (1,)), ((), ())), preferred_element_type=jnp.float32
    )


def inner_cols(left, right):
    return lax.dot_general(
        left, right, (((0,), (0,)), ((), ())), preferred_element_type=jnp.float32
    )


def layer_norm(values, gain, shift):
    center = values - jnp.mean(values, -1, keepdims=True)
    spread = jnp.mean(center * center, -1, keepdims=True)
    return center * lax.rsqrt(spread + EPSILON) * gain + shift


def gelu_tanh(values):
    return (
        0.5
        * values
        * (1.0 + jnp.tanh(0.7978845608028654 * (values + 0.044715 * values * values * values)))
    )


def sinusoid(row_count, width_all, farthest):
    distance = farthest - jnp.arange(row_count).astype(jnp.float32)
    frequency = 10000.0 ** (-jnp.arange(0, width_all, 2).astype(jnp.float32) / width_all)
    angles = distance[:, None] * frequency[None, :]
    return jnp.concatenate([jnp.sin(angles), jnp.cos(angles)], 1)


def seq_masks(seg_ids, order_row, mem_valid):
    block_ids = jnp.arange(NBLK)
    rank_of = jnp.sum(
        block_ids[None, :] * (order_row[None, :] == block_ids[:, None]).astype(jnp.int32), 1
    )
    token_rank = jnp.repeat(rank_of, BLOCK)
    valid_row = (mem_valid == 1)[None, :]
    allow_content = jnp.concatenate(
        [jnp.broadcast_to(valid_row, (L, MEM)), token_rank[None, :] <= token_rank[:, None]], 1
    )
    same_content = seg_ids[MEM:][:, None] == seg_ids[None, :]
    target_base = order_row[NBLK - 1] * BLOCK
    target_seg = lax.dynamic_slice_in_dim(seg_ids, MEM + target_base, BLOCK)
    same_query = target_seg[:, None] == seg_ids[None, :]
    positions = target_base + jnp.arange(BLOCK)
    allow_query = jnp.concatenate(
        [jnp.broadcast_to(valid_row, (BLOCK, MEM)), jnp.arange(L)[None, :] != positions[:, None]], 1
    )
    return (allow_content, same_content, allow_query, same_query, target_base)


def skew_rows(table_in, row_count, key_count):
    span_width = table_in.shape[1]
    flat_table = table_in.reshape(row_count * span_width)
    picked = flat_table[row_count - 1 : row_count - 1 + row_count * (span_width - 1)]
    return picked.reshape(row_count, span_width - 1)[:, :key_count]


def unskew_rows(grad_rows, span_width):
    row_count, key_count = grad_rows.shape
    widened = jnp.pad(grad_rows, ((0, 0), (0, span_width - 1 - key_count)))
    flat_table = jnp.pad(widened.reshape(row_count * (span_width - 1)), (row_count - 1, 1))
    return flat_table.reshape(row_count, span_width)


def block_scores(query_rows, first_row, same_seg, allowed, key_rows, rel_all, bias_three, seg_pair):
    row_count = query_rows.shape[0]
    key_count = key_rows.shape[0]
    rel_rows = lax.dynamic_slice_in_dim(
        rel_all, L - row_count - first_row, key_count + row_count - 1, 0
    )
    query_f = query_rows.astype(jnp.float32)
    query_w = (query_f + bias_three[0]).astype(jnp.bfloat16)
    query_r = (query_f + bias_three[1]).astype(jnp.bfloat16)
    query_s = query_f + bias_three[2]
    content = inner_rows(query_w, key_rows)
    position = skew_rows(inner_rows(query_r, rel_rows), row_count, key_count)
    seg_scores = jnp.dot(query_s, seg_pair.T, precision=HIGHEST)
    segment = jnp.where(same_seg, seg_scores[:, 0:1], seg_scores[:, 1:2])
    scores = jnp.where(allowed, (content + position + segment) * SCORE_SCALE, NEGATIVE)
    return (scores, query_w, query_r, query_s, rel_rows)


def block_forward(
    query_rows, first_row, same_seg, allowed, key_rows, value_rows, rel_all, bias_three, seg_pair
):
    scores = block_scores(
        query_rows, first_row, same_seg, allowed, key_rows, rel_all, bias_three, seg_pair
    )[0]
    row_max = jnp.max(scores, -1, keepdims=True)
    exp_terms = jnp.exp(scores - row_max)
    exp_total = jnp.sum(exp_terms, -1, keepdims=True)
    attn_prob = (exp_terms / exp_total).astype(jnp.bfloat16)
    return (product(attn_prob, value_rows), (row_max + jnp.log(exp_total))[:, 0])


def block_backward(
    query_rows,
    first_row,
    same_seg,
    allowed,
    key_rows,
    value_rows,
    rel_all,
    bias_three,
    seg_pair,
    log_total,
    grad_out,
    running,
):
    scores, query_w, query_r, query_s, rel_rows = block_scores(
        query_rows, first_row, same_seg, allowed, key_rows, rel_all, bias_three, seg_pair
    )
    attn_prob = jnp.exp(scores - log_total[:, None])
    grad_prob = inner_rows(grad_out, value_rows)
    grad_scores = attn_prob * (grad_prob - jnp.sum(attn_prob * grad_prob, -1, keepdims=True))
    scaled = (grad_scores * SCORE_SCALE).astype(jnp.bfloat16)
    span_width = rel_rows.shape[0]
    widened = unskew_rows(scaled, span_width)
    grad_w = product(scaled, key_rows)
    grad_r = product(widened, rel_rows)
    scaled_f = scaled.astype(jnp.float32)
    same_total = jnp.sum(jnp.where(same_seg, scaled_f, 0.0), -1)
    other_total = jnp.sum(jnp.where(same_seg, 0.0, scaled_f), -1)
    seg_grad = jnp.stack([same_total, other_total], 1)
    grad_s = jnp.dot(seg_grad, seg_pair, precision=HIGHEST)
    keys_sum, values_sum, rel_sum, bias_sum, seg_sum = running
    keys_sum = keys_sum + inner_cols(scaled, query_w)
    values_sum = values_sum + inner_cols(attn_prob.astype(jnp.bfloat16), grad_out)
    rel_start = L - query_rows.shape[0] - first_row
    current = lax.dynamic_slice_in_dim(rel_sum, rel_start, span_width, 0)
    rel_sum = lax.dynamic_update_slice_in_dim(
        rel_sum, current + inner_cols(widened, query_r), rel_start, 0
    )
    bias_sum = bias_sum + jnp.stack([jnp.sum(grad_w, 0), jnp.sum(grad_r, 0), jnp.sum(grad_s, 0)])
    seg_sum = seg_sum + jnp.dot(seg_grad.T, query_s, precision=HIGHEST)
    return (grad_w + grad_r + grad_s, (keys_sum, values_sum, rel_sum, bias_sum, seg_sum))


def head_forward(head_items, mask_set):
    content_q, query_q, key_rows, value_rows, rel_all, bias_three, seg_pair = head_items
    allow_content, same_content, allow_query, same_query, target_base = mask_set
    block_rows = min(512, L)
    out_pieces = []
    log_pieces = []
    for first_row in range(0, L, block_rows):
        stop_row = first_row + block_rows
        out_rows, log_rows = block_forward(
            content_q[first_row:stop_row],
            first_row,
            same_content[first_row:stop_row],
            allow_content[first_row:stop_row],
            key_rows,
            value_rows,
            rel_all,
            bias_three,
            seg_pair,
        )
        out_pieces.append(out_rows)
        log_pieces.append(log_rows)
    target_out, target_log = block_forward(
        query_q,
        target_base,
        same_query,
        allow_query,
        key_rows,
        value_rows,
        rel_all,
        bias_three,
        seg_pair,
    )
    return (jnp.concatenate(out_pieces, 0), jnp.concatenate(log_pieces, 0), target_out, target_log)


def head_backward(head_items, mask_set):
    (
        content_q,
        query_q,
        key_rows,
        value_rows,
        rel_all,
        bias_three,
        seg_pair,
        content_log,
        query_log,
        content_grad,
        query_grad,
    ) = head_items
    allow_content, same_content, allow_query, same_query, target_base = mask_set
    block_rows = min(512, L)
    running = (
        jnp.zeros(key_rows.shape, jnp.float32),
        jnp.zeros(value_rows.shape, jnp.float32),
        jnp.zeros(rel_all.shape, jnp.float32),
        jnp.zeros(bias_three.shape, jnp.float32),
        jnp.zeros(seg_pair.shape, jnp.float32),
    )
    grad_pieces = []
    for first_row in range(0, L, block_rows):
        stop_row = first_row + block_rows
        grad_rows, running = block_backward(
            content_q[first_row:stop_row],
            first_row,
            same_content[first_row:stop_row],
            allow_content[first_row:stop_row],
            key_rows,
            value_rows,
            rel_all,
            bias_three,
            seg_pair,
            content_log[first_row:stop_row],
            content_grad[first_row:stop_row],
            running,
        )
        grad_pieces.append(grad_rows)
    grad_target, running = block_backward(
        query_q,
        target_base,
        same_query,
        allow_query,
        key_rows,
        value_rows,
        rel_all,
        bias_three,
        seg_pair,
        query_log,
        query_grad,
        running,
    )
    return (jnp.concatenate(grad_pieces, 0), grad_target) + running


def shards(
    hidden,
    query_in,
    memory,
    segment_ids,
    block_order,
    memory_valid,
    w_query,
    w_key,
    w_value,
    w_out,
    w_rel,
    rel_biases,
    seg_embed,
    w_inner,
    b_inner,
    w_outer,
    b_outer,
    norm_gains,
    norm_biases,
    grad_hidden_out,
    grad_query_out,
):
    gathered = (
        lax.all_gather(w_query, "fsdp", axis=0, tiled=True),
        lax.all_gather(w_key, "fsdp", axis=0, tiled=True),
        lax.all_gather(w_value, "fsdp", axis=0, tiled=True),
        lax.all_gather(w_out, "fsdp", axis=0, tiled=True),
        lax.all_gather(w_inner, "fsdp", axis=0, tiled=True),
        lax.all_gather(w_outer, "fsdp", axis=0, tiled=True),
        lax.all_gather(b_inner, "fsdp", axis=0, tiled=True),
        lax.all_gather(b_outer, "fsdp", axis=0, tiled=True),
        lax.all_gather(norm_gains, "fsdp", axis=1, tiled=True),
        lax.all_gather(norm_biases, "fsdp", axis=1, tiled=True),
        lax.all_gather(w_rel, "fsdp", axis=0, tiled=True),
        lax.all_gather(rel_biases, "fsdp", axis=1, tiled=True),
        lax.all_gather(seg_embed, "fsdp", axis=1, tiled=True),
    )
    full_query, full_key, full_value, full_out, full_inner, full_outer = gathered[:6]
    inner_bias = gathered[6].astype(jnp.float32)
    outer_bias = gathered[7].astype(jnp.float32)
    gains = gathered[8].astype(jnp.float32)
    shifts = gathered[9].astype(jnp.float32)
    rel_weight = gathered[10]
    sequences, own_rows, model_width = hidden.shape
    target_rows = query_in.shape[1]
    memory_rows = memory.shape[1]
    content_rows = sequences * own_rows
    flat_hidden = hidden.reshape(content_rows, model_width)
    flat_query = query_in.reshape(sequences * target_rows, model_width)
    flat_memory = memory.reshape(sequences * memory_rows, model_width)
    pair_count = lax.axis_size("seq")
    head_width = model_width // pair_count

    def project(rows_in, weight, per_seq):
        return (
            product(rows_in, weight).astype(jnp.bfloat16).reshape(sequences, per_seq, model_width)
        )

    head_q, head_k, head_v, head_km, head_vm, head_qg = (
        lax.all_to_all(
            project(flat_hidden, full_query, own_rows),
            "seq",
            split_axis=2,
            concat_axis=1,
            tiled=True,
        ),
        lax.all_to_all(
            project(flat_hidden, full_key, own_rows), "seq", split_axis=2, concat_axis=1, tiled=True
        ),
        lax.all_to_all(
            project(flat_hidden, full_value, own_rows),
            "seq",
            split_axis=2,
            concat_axis=1,
            tiled=True,
        ),
        lax.all_to_all(
            project(flat_memory, full_key, memory_rows),
            "seq",
            split_axis=2,
            concat_axis=1,
            tiled=True,
        ),
        lax.all_to_all(
            project(flat_memory, full_value, memory_rows),
            "seq",
            split_axis=2,
            concat_axis=1,
            tiled=True,
        ),
        lax.all_to_all(
            project(flat_query, full_query, target_rows),
            "seq",
            split_axis=2,
            concat_axis=1,
            tiled=True,
        ),
    )
    local_heads = head_width // DH
    key_count = MEM + L
    rel_count = MEM + 2 * L - 1
    pos_table = sinusoid(rel_count, model_width, MEM + L - 1).astype(jnp.bfloat16)
    rel_heads = (
        product(pos_table, rel_weight)
        .astype(jnp.bfloat16)
        .reshape(rel_count, local_heads, DH)
        .transpose(1, 0, 2)
    )
    bias_heads = gathered[11].astype(jnp.float32).reshape(3, local_heads, DH).transpose(1, 0, 2)
    seg_heads = gathered[12].astype(jnp.float32).reshape(2, local_heads, DH).transpose(1, 0, 2)

    def heads_first(values, count):
        return values.reshape(sequences, count, local_heads, DH).transpose(0, 2, 1, 3)

    def tokens_last(values, count):
        return (
            values.transpose(0, 2, 1, 3).reshape(sequences, count, head_width).astype(jnp.bfloat16)
        )

    content_q = heads_first(head_q, L)
    query_q = heads_first(head_qg, BLOCK)
    key_heads = heads_first(jnp.concatenate([head_km, head_k], 1), key_count)
    value_heads = heads_first(jnp.concatenate([head_vm, head_v], 1), key_count)

    def seq_forward(seq_items):
        seq_content, seq_query, seq_keys, seq_values, seg_ids, order_row, mem_valid = seq_items
        mask_set = seq_masks(seg_ids, order_row, mem_valid)
        return lax.map(
            lambda head_items: head_forward(head_items, mask_set),
            (seq_content, seq_query, seq_keys, seq_values, rel_heads, bias_heads, seg_heads),
        )

    content_att, content_log, query_att, query_log = lax.map(
        seq_forward,
        (content_q, query_q, key_heads, value_heads, segment_ids, block_order, memory_valid),
    )
    back_h, back_g = (
        lax.all_to_all(tokens_last(content_att, L), "seq", split_axis=1, concat_axis=2, tiled=True),
        lax.all_to_all(
            tokens_last(query_att, BLOCK), "seq", split_axis=1, concat_axis=2, tiled=True
        ),
    )
    attn_rows = jnp.concatenate(
        [
            back_h.reshape(content_rows, model_width),
            back_g.reshape(sequences * target_rows, model_width),
        ],
        0,
    )
    resid_rows = jnp.concatenate([flat_hidden, flat_query], 0).astype(jnp.float32)
    first_sum = product(attn_rows, full_out) + resid_rows
    first_norm = layer_norm(first_sum, gains[0], shifts[0])
    first_low = first_norm.astype(jnp.bfloat16)
    hidden_pre = product(first_low, full_inner) + inner_bias
    activation = gelu_tanh(hidden_pre).astype(jnp.bfloat16)
    second_sum = product(activation, full_outer) + outer_bias + first_norm
    result = layer_norm(second_sum, gains[1], shifts[1])
    hidden_out = (
        result[:content_rows].reshape(sequences, own_rows, model_width).astype(jnp.bfloat16)
    )
    query_out = (
        result[content_rows:].reshape(sequences, target_rows, model_width).astype(jnp.bfloat16)
    )
    refreshed = (full_query, full_key, full_value, full_out, full_inner, full_outer)
    back_query, back_key, back_value, back_out, back_inner, back_outer = refreshed
    grad_rows = jnp.concatenate(
        [
            grad_hidden_out.reshape(content_rows, model_width),
            grad_query_out.reshape(sequences * target_rows, model_width),
        ],
        0,
    ).astype(jnp.float32)
    second_pull = jax.vjp(layer_norm, second_sum, gains[1], shifts[1])[1]
    grad_second, grad_gain_two, grad_shift_two = second_pull(grad_rows)
    grad_outer_low = grad_second.astype(jnp.bfloat16)
    grad_b_outer = jnp.sum(grad_outer_low.astype(jnp.float32), 0)
    grad_w_outer = inner_cols(activation, grad_outer_low)
    gelu_pull = jax.vjp(gelu_tanh, hidden_pre)[1]
    grad_pre = gelu_pull(inner_rows(grad_outer_low, back_outer))[0].astype(jnp.bfloat16)
    grad_b_inner = jnp.sum(grad_pre.astype(jnp.float32), 0)
    grad_w_inner = inner_cols(first_low, grad_pre)
    grad_first = grad_second + inner_rows(grad_pre, back_inner)
    first_pull = jax.vjp(layer_norm, first_sum, gains[0], shifts[0])[1]
    grad_sum_one, grad_gain_one, grad_shift_one = first_pull(grad_first)
    grad_mixed = grad_sum_one.astype(jnp.bfloat16)
    grad_w_out = inner_cols(attn_rows, grad_mixed)
    grad_attn = inner_rows(grad_mixed, back_out).astype(jnp.bfloat16)
    grad_h_heads, grad_g_heads = (
        lax.all_to_all(
            grad_attn[:content_rows].reshape(sequences, own_rows, model_width),
            "seq",
            split_axis=2,
            concat_axis=1,
            tiled=True,
        ),
        lax.all_to_all(
            grad_attn[content_rows:].reshape(sequences, target_rows, model_width),
            "seq",
            split_axis=2,
            concat_axis=1,
            tiled=True,
        ),
    )

    def seq_backward(seq_items):
        (
            seq_content,
            seq_query,
            seq_keys,
            seq_values,
            seg_ids,
            order_row,
            mem_valid,
            seq_log,
            seq_query_log,
            seq_grad,
            seq_query_grad,
        ) = seq_items
        mask_set = seq_masks(seg_ids, order_row, mem_valid)
        return lax.map(
            lambda head_items: head_backward(head_items, mask_set),
            (
                seq_content,
                seq_query,
                seq_keys,
                seq_values,
                rel_heads,
                bias_heads,
                seg_heads,
                seq_log,
                seq_query_log,
                seq_grad,
                seq_query_grad,
            ),
        )

    grad_content_q, grad_query_q, grad_keys, grad_values, grad_rel, grad_bias, grad_seg = lax.map(
        seq_backward,
        (
            content_q,
            query_q,
            key_heads,
            value_heads,
            segment_ids,
            block_order,
            memory_valid,
            content_log,
            query_log,
            heads_first(grad_h_heads, L),
            heads_first(grad_g_heads, BLOCK),
        ),
    )
    rel_low = grad_rel.astype(jnp.bfloat16)
    grad_rel_weight = jnp.einsum(
        "rd,shrk->dhk", pos_table, rel_low, preferred_element_type=jnp.float32
    ).reshape(model_width, head_width)
    grad_bias_part = jnp.sum(grad_bias, 0).transpose(1, 0, 2).reshape(3, head_width)
    grad_seg_part = jnp.sum(grad_seg, 0).transpose(1, 0, 2).reshape(2, head_width)
    grad_w_rel, grad_rel_biases, grad_seg_embed = (
        lax.psum_scatter(grad_rel_weight, "fsdp", scatter_dimension=0, tiled=True),
        lax.psum_scatter(grad_bias_part, "fsdp", scatter_dimension=1, tiled=True),
        lax.psum_scatter(grad_seg_part, "fsdp", scatter_dimension=1, tiled=True),
    )
    keys_low = tokens_last(grad_keys, key_count)
    values_low = tokens_last(grad_values, key_count)
    query_low = tokens_last(grad_content_q, L)
    target_low = tokens_last(grad_query_q, BLOCK)
    grad_gains = jnp.stack([grad_gain_one, grad_gain_two], 0)
    grad_shifts = jnp.stack([grad_shift_one, grad_shift_two], 0)
    tok_query, tok_key, tok_value, tok_mem_key, tok_mem_value, tok_target = (
        lax.all_to_all(query_low, "seq", split_axis=1, concat_axis=2, tiled=True),
        lax.all_to_all(keys_low[:, MEM:], "seq", split_axis=1, concat_axis=2, tiled=True),
        lax.all_to_all(values_low[:, MEM:], "seq", split_axis=1, concat_axis=2, tiled=True),
        lax.all_to_all(keys_low[:, :MEM], "seq", split_axis=1, concat_axis=2, tiled=True),
        lax.all_to_all(values_low[:, :MEM], "seq", split_axis=1, concat_axis=2, tiled=True),
        lax.all_to_all(target_low, "seq", split_axis=1, concat_axis=2, tiled=True),
    )
    flat_dq = tok_query.reshape(content_rows, model_width)
    flat_dk = tok_key.reshape(content_rows, model_width)
    flat_dv = tok_value.reshape(content_rows, model_width)
    flat_dkm = tok_mem_key.reshape(sequences * memory_rows, model_width)
    flat_dvm = tok_mem_value.reshape(sequences * memory_rows, model_width)
    flat_dqg = tok_target.reshape(sequences * target_rows, model_width)
    grad_w_query = inner_cols(flat_hidden, flat_dq) + inner_cols(flat_query, flat_dqg)
    grad_w_key = inner_cols(flat_hidden, flat_dk) + inner_cols(flat_memory, flat_dkm)
    grad_w_value = inner_cols(flat_hidden, flat_dv) + inner_cols(flat_memory, flat_dvm)
    grad_hidden = (
        grad_sum_one[:content_rows]
        + inner_rows(flat_dq, back_query)
        + inner_rows(flat_dk, back_key)
        + inner_rows(flat_dv, back_value)
    )
    grad_query = grad_sum_one[content_rows:] + inner_rows(flat_dqg, back_query)
    shares = (
        lax.psum_scatter(grad_w_query, ("seq", "fsdp"), scatter_dimension=0, tiled=True),
        lax.psum_scatter(grad_w_key, ("seq", "fsdp"), scatter_dimension=0, tiled=True),
        lax.psum_scatter(grad_w_value, ("seq", "fsdp"), scatter_dimension=0, tiled=True),
        lax.psum_scatter(grad_w_out, ("seq", "fsdp"), scatter_dimension=0, tiled=True),
        lax.psum_scatter(grad_w_inner, ("seq", "fsdp"), scatter_dimension=0, tiled=True),
        lax.psum_scatter(grad_w_outer, ("seq", "fsdp"), scatter_dimension=0, tiled=True),
        lax.psum_scatter(grad_b_inner, ("seq", "fsdp"), scatter_dimension=0, tiled=True),
        lax.psum_scatter(grad_b_outer, ("seq", "fsdp"), scatter_dimension=0, tiled=True),
        lax.psum_scatter(grad_gains, ("seq", "fsdp"), scatter_dimension=1, tiled=True),
        lax.psum_scatter(grad_shifts, ("seq", "fsdp"), scatter_dimension=1, tiled=True),
    )
    out_query, out_key, out_value, out_out = (shares[0], shares[1], shares[2], shares[3])
    out_inner, out_outer, out_b_inner, out_b_outer = (shares[4], shares[5], shares[6], shares[7])
    out_gains, out_shifts = (shares[8], shares[9])
    return (
        hidden_out,
        query_out,
        grad_hidden.reshape(sequences, own_rows, model_width),
        grad_query.reshape(sequences, target_rows, model_width),
        out_query,
        out_key,
        out_value,
        out_out,
        grad_w_rel,
        grad_rel_biases,
        grad_seg_embed,
        out_inner,
        out_b_inner,
        out_outer,
        out_b_outer,
        out_gains,
        out_shifts,
    )


def solution(mesh):
    in_specs = (
        P("fsdp", "seq", None),
        P("fsdp", "seq", None),
        P("fsdp", "seq", None),
        P("fsdp", None),
        P("fsdp", None),
        P("fsdp", None),
        P("fsdp", None),
        P("fsdp", None),
        P("fsdp", None),
        P("fsdp", None),
        P("fsdp", "seq"),
        P(None, ("seq", "fsdp")),
        P(None, ("seq", "fsdp")),
        P("fsdp", None),
        P("fsdp"),
        P("fsdp", None),
        P("fsdp"),
        P(None, "fsdp"),
        P(None, "fsdp"),
        P("fsdp", "seq", None),
        P("fsdp", "seq", None),
    )
    out_specs = (
        P("fsdp", "seq", None),
        P("fsdp", "seq", None),
        P("fsdp", "seq", None),
        P("fsdp", "seq", None),
        P(("seq", "fsdp"), None),
        P(("seq", "fsdp"), None),
        P(("seq", "fsdp"), None),
        P(("seq", "fsdp"), None),
        P("fsdp", "seq"),
        P(None, ("seq", "fsdp")),
        P(None, ("seq", "fsdp")),
        P(("seq", "fsdp"), None),
        P(("seq", "fsdp")),
        P(("seq", "fsdp"), None),
        P(("seq", "fsdp")),
        P(None, ("seq", "fsdp")),
        P(None, ("seq", "fsdp")),
    )
    return jax.shard_map(shards, mesh=mesh, in_specs=in_specs, out_specs=out_specs, check_vma=False)
```

profile of v0, /device:TPU:0, one launch (start us, length us, event | category | flops | bytes accessed | tf_op | source)
XLA Modules:
  0.0 2797.7 jit_solution(6613328634765316263)
XLA Ops:
  14.0 25.6 all_gather.42
  41.9 17.5 all-gather
  59.4 18.7 all-gather.1
  78.2 14.5 fusion.300
  117.4 14.3 all-gather.15.cloned.1.call-done
  233.7 495.9 %while.78 = (s32[]{:T(128)}, bf16[6,1024,64]{1,2,0:T(8,128)(2,1)}, f32[6,1024]{1,0:T(8,128)}, bf16[6,256,64]{1,2,0:T(8,128)(2,1)}, f32[6,256]{1,0:T(8,128)}, /*i...) while((s32[]{:T(128)}, bf16[6,1024,64]{1,2,0:T(8,128)(2,1)}, ...), condition=%wide.region_8.9_spmd.clone, body=%wide.region_1.8_spmd.clone.sunk | while | flops 790462208 | bytes 128070920 | solution.py:386
  250.7 7.8 reshape.1218
  282.1 7.8 reshape.1216
  333.4 7.8 reshape.1218
  364.7 7.8 reshape.1216
  415.9 7.8 reshape.1218
  447.2 7.8 reshape.1216
  498.4 7.8 reshape.1218
  529.7 7.8 reshape.1216
  580.9 7.8 reshape.1218
  612.2 7.8 reshape.1216
  663.5 7.8 reshape.1218
  694.8 7.8 reshape.1216
  737.0 19.2 all-gather.2
  768.6 17.3 all-gather.3
  788.4 31.6 %all-reduce.17 = (bf16[768]{0:T(1024)(128)(2,1)S(1)}, bf16[3072]{0:T(1024)(128)(2,1)S(1)}) all-reduce(bf16[768]{0:T(1024)(128)(2,1)S(1)} %dynamic-update-slice.1, bf16[3072]{0:T(1024)(128)(2,1)S(1)} %dynamic-update-slice), channel_id=1, replica_groups=mesh['seq'=2,'fsdp'=16] {'fsdp'}, use_global_device_ids=true, to_apply=%add.8 | all-reduce | flops 3840 | bytes 15360
  829.3 8.2 fusion.344
  837.5 9.7 fusion.367
  852.6 10.1 convert_reduce_fusion
  891.3 7.4 all-to-all-done.8
  905.5 1121.1 %while.79 = (s32[]{:T(128)}, bf16[6,1024,64]{1,2,0:T(8,128)(2,1)}, bf16[6,256,64]{1,2,0:T(8,128)(2,1)}, bf16[6,1408,64]{1,2,0:T(8,128)(2,1)}, bf16[6,1408,64]{1,...) while((s32[]{:T(128)}, bf16[6,1024,64]{1,2,0:T(8,128)(2,1)}, ...), condition=%wide.region_36.37_spmd.clone, body=%wide.region_17.36_spmd.clone.sunk | while | flops 2113194752 | bytes 328340608 | solution.py:478
  922.2 7.8 reshape.1224
  933.8 6.8 multiply_reduce_fusion.11
  945.6 6.7 reshape.1221
  957.4 7.8 reshape.1222
  1052.8 6.8 reshape.1226
  1107.9 7.8 reshape.1224
  1119.5 6.8 multiply_reduce_fusion.11
  1143.1 7.8 reshape.1222
  1238.6 6.8 reshape.1226
  1293.4 7.8 reshape.1224
  1305.0 6.8 multiply_reduce_fusion.11
  1316.8 6.9 reshape.1221
  1328.8 7.8 reshape.1222
  1424.1 7.0 reshape.1226
  1479.2 7.8 reshape.1224
  1490.7 6.8 multiply_reduce_fusion.11
  1514.3 7.8 reshape.1222
  1609.8 6.8 reshape.1226
  1664.9 7.8 reshape.1224
  1676.5 6.8 multiply_reduce_fusion.11
  1700.0 7.8 reshape.1222
  1795.5 6.8 reshape.1226
  1850.4 7.8 reshape.1224
  1862.0 6.8 multiply_reduce_fusion.11
  1873.8 6.9 reshape.1221
  1885.8 7.8 reshape.1222
  1981.1 7.0 reshape.1226
  2097.1 7.3 reduce.21
  2146.7 7.3 reduce.22
  2163.3 6.8 all-to-all-done.10
  2185.0 10.4 fusion.342
  2196.6 12.0 fusion.346
  2209.6 40.1 %all-reduce.15 = (f32[3072]{0:T(1024)S(1)}, f32[768]{0:T(1024)S(1)}, f32[2,768]{1,0:T(2,128)S(1)}, f32[2,768]{1,0:T(2,128)S(1)}) all-reduce(f32[3072]{0:T(1024)S(1)} %copy-done.99, f32[768]{0:T(1024)S(1)} %copy-done.95, f32[2,768]{1,0:T(2,128)S(1)} %pad_maximum_fusion.17, ...), channel_id=10, replica_groups=mesh['seq'=2,'fsdp'=16] {'seq','fsdp'}, use_global_device_ids=true, to_apply=%region_46.47.clone | all-reduce | flops 6912 | bytes 55296
  2256.0 32.6 %all-reduce.16 = (f32[3,384]{1,0:T(4,128)S(1)}, f32[2,384]{1,0:T(2,128)S(1)}) all-reduce(f32[3,384]{1,0:T(4,128)S(1)} %reshape.1087, f32[2,384]{1,0:T(2,128)S(1)} %reshape.1088), channel_id=7, replica_groups=mesh['seq'=2,'fsdp'=16] {'fsdp'}, use_global_device_ids=true, to_apply=%region_42.43.clone | all-reduce | flops 1920 | bytes 15360
  2299.2 103.7 %reduce-scatter.28.cloned.1.call-done = f32[24,768]{1,0:T(8,128)} async-done(((f32[768,768]{1,0:T(8,128)}), f32[24,768]{1,0:T(8,128)}) %reduce-scatter.28.cloned.1.call-update) | async-done | bytes 73744
  2402.9 104.8 %reduce-scatter.26.cloned.1.call-done = f32[24,768]{1,0:T(8,128)} async-done(((f32[768,768]{1,0:T(8,128)}), f32[24,768]{1,0:T(8,128)}) %reduce-scatter.26.cloned.1.call-update) | async-done | bytes 73744
  2507.7 141.0 %reduce-scatter.22.cloned.1.call-done = f32[24,3072]{1,0:T(8,128)} async-done(((f32[768,3072]{1,0:T(8,128)}), f32[24,3072]{1,0:T(8,128)}) %reduce-scatter.22.cloned.1.call-update) | async-done | bytes 294928 | tf_op jit(solution)/shard_map/reduce_scatter | solution.py:557
  2648.7 142.2 %reduce-scatter.24.cloned.1.call-done = f32[96,768]{1,0:T(8,128)} async-done(((f32[3072,768]{1,0:T(8,128)}), f32[96,768]{1,0:T(8,128)}) %reduce-scatter.24.cloned.1.call-update) | async-done | bytes 294928 | tf_op jit(solution)/shard_map/reduce_scatter | solution.py:558
  (1663 shorter events, 1673.1 us)
Async XLA Ops:
  7.2 100.1 %copy-start = (bf16[1,192,768]{2,1,0:T(8,128)(2,1)S(1)}, bf16[1,192,768]{2,1,0:T(8,128)(2,1)}, u32[]{:S(2)}) copy-start(bf16[1,192,768]{2,1,0:T(8,128)(2,1)} %param.27) | copy-start | bytes 884740
  7.2 34.7 %copy-start.107 = (bf16[3,24]{1,0:T(4,128)(2,1)S(1)}, bf16[3,24]{1,0:T(4,128)(2,1)}, u32[]{:S(2)}) copy-start(bf16[3,24]{1,0:T(4,128)(2,1)} %param.36) | copy-start | bytes 436
  7.2 52.2 %copy-start.108 = (bf16[2,24]{1,0:T(2,128)(2,1)S(1)}, bf16[2,24]{1,0:T(2,128)(2,1)}, u32[]{:S(2)}) copy-start(bf16[2,24]{1,0:T(2,128)(2,1)} %param.37) | copy-start | bytes 292
  7.2 91.3 %all-gather.11.cloned.1.call-start = ((), (), s32[]{:S(2)}) async-start(), calls=%async_computation.23 | async-start | bytes 1253376 | tf_op jit(solution)/shard_map/all_gather | solution.py:282
  8.0 99.3 %all-gather.13.cloned.1.call-start = ((), (), s32[]{:S(2)}) async-start(), calls=%async_computation.24 | async-start | bytes 1253376 | tf_op jit(solution)/shard_map/all_gather | solution.py:283
  8.7 123.0 %all-gather.15.cloned.1.call-start = ((), (), s32[]{:S(2)}) async-start(), calls=%async_computation.25 | async-start | bytes 1253376 | tf_op jit(solution)/shard_map/all_gather | solution.py:284
  9.4 816.9 %all-gather.17.cloned.1.call-start = ((), (), s32[]{:S(2)}) async-start(), calls=%async_computation.26 | async-start | bytes 1253376 | tf_op jit(solution)/shard_map/all_gather | solution.py:285
  10.0 819.3 %all-gather.19.cloned.1.call-start = ((), (), s32[]{:S(2)}) async-start(), calls=%async_computation.27 | async-start | bytes 5013504 | tf_op jit(solution)/shard_map/all_gather | solution.py:286
  10.6 826.9 %all-gather.21.cloned.1.call-start = ((), (), s32[]{:S(2)}) async-start(), calls=%async_computation.28 | async-start | bytes 5013504 | tf_op jit(solution)/shard_map/all_gather | solution.py:287
  40.4 55.4 %copy-start.44 = (s32[1408]{0:T(1024)}, s32[1408]{0:T(1024)S(1)}, u32[]{:S(2)}) copy-start(s32[1408]{0:T(1024)S(1)} %reduce.2) | copy-start | bytes 16900
  103.6 10.4 all-to-all-start.5
  113.9 24.4 all-to-all-start.1
  138.4 19.6 all-to-all-start.3
  158.0 18.7 all-to-all-start.2
  176.7 34.2 %all-to-all-start.4 = ((bf16[2,2,98304]{2,1,0:T(2,128)(2,1)}), bf16[2,2,98304]{2,1,0:T(2,128)(2,1)}, u32[]{:S(2)}, u32[]{:S(2)}) async-start(bf16[2,2,98304]{2,1,0:T(2,128)(2,1)} %reshape.1171), calls=%async_computation.4 | async-start | bytes 1572864 | tf_op jit(solution)/shard_map/all_to_all | solution.py:328
  210.9 16.4 all-to-all-start
  235.1 23.4 copy-start.75
  729.6 26.6 copy-start.34
  733.6 31.4 %all-to-all-start.7 = ((bf16[2,2,24576]{2,1,0:T(2,128)(2,1)}), bf16[2,2,24576]{2,1,0:T(2,128)(2,1)S(1)}, u32[]{:S(2)}, u32[]{:S(2)}) async-start(bf16[2,2,24576]{2,1,0:T(2,128)(2,1)} %reshape.1177), calls=%async_computation.7 | async-start | bytes 393216 | tf_op jit(solution)/shard_map/all_to_all | solution.py:397
  763.9 24.0 copy-start.112
  763.9 24.3 copy-start.113
  764.9 55.1 %copy-start.52 = (bf16[2,2,24576]{2,1,0:T(2,128)(2,1)}, bf16[2,2,24576]{2,1,0:T(2,128)(2,1)S(1)}, u32[]{:S(2)}) copy-start(bf16[2,2,24576]{2,1,0:T(2,128)(2,1)S(1)} %all-to-all-done.7) | copy-start | bytes 589828
  764.9 57.3 %all-to-all-start.6 = ((bf16[2,2,98304]{2,1,0:T(2,128)(2,1)}), bf16[2,2,98304]{2,1,0:T(2,128)(2,1)S(1)}, u32[]{:S(2)}, u32[]{:S(2)}) async-start(bf16[2,2,98304]{2,1,0:T(2,128)(2,1)} %reshape.1179), calls=%async_computation.6 | async-start | bytes 1572864 | tf_op jit(solution)/shard_map/all_to_all | solution.py:396
  820.0 32.5 %copy-start.100 = (f32[3072]{0:T(1024)}, f32[3072]{0:T(1024)S(1)}, u32[]{:S(2)}) copy-start(f32[3072]{0:T(1024)S(1)} %convert_element_type.587) | copy-start | bytes 36868
  820.1 46.9 %copy-start.63 = (f32[768]{0:T(1024)}, f32[768]{0:T(1024)S(1)}, u32[]{:S(2)}) copy-start(f32[768]{0:T(1024)S(1)} %get-tuple-element.1524) | copy-start | bytes 9220
  828.9 38.1 %copy-start.20 = (f32[640,768]{1,0:T(8,128)}, f32[640,768]{1,0:T(8,128)S(1)}, u32[]{:S(2)}) copy-start(f32[640,768]{1,0:T(8,128)S(1)} %get-tuple-element.1518) | copy-start | bytes 5898244
  828.9 38.1 %copy-start.58 = (f32[640]{0:T(1024)}, f32[640]{0:T(1024)S(1)}, u32[]{:S(2)}) copy-start(f32[640]{0:T(1024)S(1)} %broadcast_multiply_fusion.1) | copy-start | bytes 7684
  829.3 37.8 %copy-start.65 = (f32[640]{0:T(1024)}, f32[640]{0:T(1024)S(1)}, u32[]{:S(2)}) copy-start(f32[640]{0:T(1024)S(1)} %fusion.325) | copy-start | bytes 7684
  873.4 12.0 all-to-all-start.9
  885.5 13.2 all-to-all-start.8
  889.0 1407.9 %reduce-scatter.20.cloned.1.call-start = ((), (), s32[]{:S(2)}) async-start(), calls=%async_computation.30 | async-start | bytes 1253376 | tf_op jit(solution)/shard_map/reduce_scatter | solution.py:518
  905.7 59.5 %copy-start.27 = (bf16[6,1024,64]{1,2,0:T(8,128)(2,1)}, bf16[6,1024,64]{1,2,0:T(8,128)(2,1)S(1)}, u32[]{:S(2)}) copy-start(bf16[6,1024,64]{1,2,0:T(8,128)(2,1)S(1)} %get-tuple-element.2060) | copy-start | bytes 2359300 | tf_op jit(solution)/shard_map/while/body/eval_jaxpr/while
  905.7 91.3 %copy-start.21 = (pred[256,1408]{1,0:T(32,128)(4,1)}, pred[256,1408]{1,0:T(32,128)(4,1)S(1)}, u32[]{:S(2)}) copy-start(pred[256,1408]{1,0:T(32,128)(4,1)S(1)} %get-tuple-element.2064) | copy-start | bytes 1081348 | tf_op jit(solution)/shard_map/while/body/eval_jaxpr/while
  906.9 33.7 %copy-start.60 = (f32[64]{0:T(128)}, f32[64]{0:T(128)S(1)}, u32[]{:S(2)}) copy-start(f32[64]{0:T(128)S(1)} %get-tuple-element.1871) | copy-start | bytes 772 | tf_op jit(solution)/shard_map/while/body/eval_jaxpr/while
  1091.4 59.4 %copy-start.27 = (bf16[6,1024,64]{1,2,0:T(8,128)(2,1)}, bf16[6,1024,64]{1,2,0:T(8,128)(2,1)S(1)}, u32[]{:S(2)}) copy-start(bf16[6,1024,64]{1,2,0:T(8,128)(2,1)S(1)} %get-tuple-element.2060) | copy-start | bytes 2359300 | tf_op jit(solution)/shard_map/while/body/eval_jaxpr/while
  1091.4 91.0 %copy-start.21 = (pred[256,1408]{1,0:T(32,128)(4,1)}, pred[256,1408]{1,0:T(32,128)(4,1)S(1)}, u32[]{:S(2)}) copy-start(pred[256,1408]{1,0:T(32,128)(4,1)S(1)} %get-tuple-element.2064) | copy-start | bytes 1081348 | tf_op jit(solution)/shard_map/while/body/eval_jaxpr/while
  1092.7 33.7 %copy-start.60 = (f32[64]{0:T(128)}, f32[64]{0:T(128)S(1)}, u32[]{:S(2)}) copy-start(f32[64]{0:T(128)S(1)} %get-tuple-element.1871) | copy-start | bytes 772 | tf_op jit(solution)/shard_map/while/body/eval_jaxpr/while
  1276.9 59.7 %copy-start.27 = (bf16[6,1024,64]{1,2,0:T(8,128)(2,1)}, bf16[6,1024,64]{1,2,0:T(8,128)(2,1)S(1)}, u32[]{:S(2)}) copy-start(bf16[6,1024,64]{1,2,0:T(8,128)(2,1)S(1)} %get-tuple-element.2060) | copy-start | bytes 2359300 | tf_op jit(solution)/shard_map/while/body/eval_jaxpr/while
  1276.9 91.2 %copy-start.21 = (pred[256,1408]{1,0:T(32,128)(4,1)}, pred[256,1408]{1,0:T(32,128)(4,1)S(1)}, u32[]{:S(2)}) copy-start(pred[256,1408]{1,0:T(32,128)(4,1)S(1)} %get-tuple-element.2064) | copy-start | bytes 1081348 | tf_op jit(solution)/shard_map/while/body/eval_jaxpr/while
  1278.2 33.7 %copy-start.60 = (f32[64]{0:T(128)}, f32[64]{0:T(128)S(1)}, u32[]{:S(2)}) copy-start(f32[64]{0:T(128)S(1)} %get-tuple-element.1871) | copy-start | bytes 772 | tf_op jit(solution)/shard_map/while/body/eval_jaxpr/while
  1462.6 59.5 %copy-start.27 = (bf16[6,1024,64]{1,2,0:T(8,128)(2,1)}, bf16[6,1024,64]{1,2,0:T(8,128)(2,1)S(1)}, u32[]{:S(2)}) copy-start(bf16[6,1024,64]{1,2,0:T(8,128)(2,1)S(1)} %get-tuple-element.2060) | copy-start | bytes 2359300 | tf_op jit(solution)/shard_map/while/body/eval_jaxpr/while
  1462.7 91.3 %copy-start.21 = (pred[256,1408]{1,0:T(32,128)(4,1)}, pred[256,1408]{1,0:T(32,128)(4,1)S(1)}, u32[]{:S(2)}) copy-start(pred[256,1408]{1,0:T(32,128)(4,1)S(1)} %get-tuple-element.2064) | copy-start | bytes 1081348 | tf_op jit(solution)/shard_map/while/body/eval_jaxpr/while
  1463.9 33.7 %copy-start.60 = (f32[64]{0:T(128)}, f32[64]{0:T(128)S(1)}, u32[]{:S(2)}) copy-start(f32[64]{0:T(128)S(1)} %get-tuple-element.1871) | copy-start | bytes 772 | tf_op jit(solution)/shard_map/while/body/eval_jaxpr/while
  1648.4 59.4 %copy-start.27 = (bf16[6,1024,64]{1,2,0:T(8,128)(2,1)}, bf16[6,1024,64]{1,2,0:T(8,128)(2,1)S(1)}, u32[]{:S(2)}) copy-start(bf16[6,1024,64]{1,2,0:T(8,128)(2,1)S(1)} %get-tuple-element.2060) | copy-start | bytes 2359300 | tf_op jit(solution)/shard_map/while/body/eval_jaxpr/while
  1648.4 91.0 %copy-start.21 = (pred[256,1408]{1,0:T(32,128)(4,1)}, pred[256,1408]{1,0:T(32,128)(4,1)S(1)}, u32[]{:S(2)}) copy-start(pred[256,1408]{1,0:T(32,128)(4,1)S(1)} %get-tuple-element.2064) | copy-start | bytes 1081348 | tf_op jit(solution)/shard_map/while/body/eval_jaxpr/while
  1649.6 33.7 %copy-start.60 = (f32[64]{0:T(128)}, f32[64]{0:T(128)S(1)}, u32[]{:S(2)}) copy-start(f32[64]{0:T(128)S(1)} %get-tuple-element.1871) | copy-start | bytes 772 | tf_op jit(solution)/shard_map/while/body/eval_jaxpr/while
  1833.9 59.7 %copy-start.27 = (bf16[6,1024,64]{1,2,0:T(8,128)(2,1)}, bf16[6,1024,64]{1,2,0:T(8,128)(2,1)S(1)}, u32[]{:S(2)}) copy-start(bf16[6,1024,64]{1,2,0:T(8,128)(2,1)S(1)} %get-tuple-element.2060) | copy-start | bytes 2359300 | tf_op jit(solution)/shard_map/while/body/eval_jaxpr/while
  1833.9 91.2 %copy-start.21 = (pred[256,1408]{1,0:T(32,128)(4,1)}, pred[256,1408]{1,0:T(32,128)(4,1)S(1)}, u32[]{:S(2)}) copy-start(pred[256,1408]{1,0:T(32,128)(4,1)S(1)} %get-tuple-element.2064) | copy-start | bytes 1081348 | tf_op jit(solution)/shard_map/while/body/eval_jaxpr/while
  1835.2 33.7 %copy-start.60 = (f32[64]{0:T(128)}, f32[64]{0:T(128)S(1)}, u32[]{:S(2)}) copy-start(f32[64]{0:T(128)S(1)} %get-tuple-element.1871) | copy-start | bytes 772 | tf_op jit(solution)/shard_map/while/body/eval_jaxpr/while
  2032.7 264.2 %reduce-scatter.18.cloned.1.call-start = ((), (), s32[]{:S(2)}) async-start(), calls=%async_computation.29 | async-start | bytes 2433024 | tf_op jit(solution)/shard_map/reduce_scatter | solution.py:556
  2040.2 14.9 all-to-all-start.15
  2055.1 11.5 all-to-all-start.12
  2058.6 240.6 %reduce-scatter.30.cloned.1.call-start = ((), (), s32[]{:S(2)}) async-start(), calls=%async_computation.35 | async-start | bytes 2433024
  2086.8 19.6 all-to-all-start.14
  2106.4 12.4 all-to-all-start.11
  2110.7 292.2 %reduce-scatter.28.cloned.1.call-start = ((), (), s32[]{:S(2)}) async-start(), calls=%async_computation.34 | async-start | bytes 2433024
  2138.5 17.5 all-to-all-start.13
  2156.0 14.1 all-to-all-start.10
  2160.4 347.4 %reduce-scatter.26.cloned.1.call-start = ((), (), s32[]{:S(2)}) async-start(), calls=%async_computation.33 | async-start | bytes 2433024
  2184.4 464.4 %reduce-scatter.22.cloned.1.call-start = ((), (), s32[]{:S(2)}) async-start(), calls=%async_computation.31 | async-start | bytes 9732096 | tf_op jit(solution)/shard_map/reduce_scatter | solution.py:557
  2195.5 595.4 %reduce-scatter.24.cloned.1.call-start = ((), (), s32[]{:S(2)}) async-start(), calls=%async_computation.32 | async-start | bytes 9732096 | tf_op jit(solution)/shard_map/reduce_scatter | solution.py:558
  2208.7 47.2 %copy-start.102 = (f32[6,3,64]{2,1,0:T(4,128)S(1)}, f32[6,3,64]{2,1,0:T(4,128)}, u32[]{:S(2)}) copy-start(f32[6,3,64]{2,1,0:T(4,128)} %get-tuple-element.2098) | copy-start | bytes 13828
  2208.7 47.3 %copy-start.103 = (f32[6,2,64]{2,1,0:T(2,128)S(1)}, f32[6,2,64]{2,1,0:T(2,128)}, u32[]{:S(2)}) copy-start(f32[6,2,64]{2,1,0:T(2,128)} %get-tuple-element.2099) | copy-start | bytes 9220
  2208.7 81.3 %copy-start.30 = (bf16[768,768]{1,0:T(8,128)(2,1)S(1)}, bf16[768,768]{1,0:T(8,128)(2,1)}, u32[]{:S(2)}) copy-start(bf16[768,768]{1,0:T(8,128)(2,1)} %all-gather.11.cloned.1.call-done) | copy-start | bytes 3538948
  (350 other events, 1158.5 us)
Sparse Core Ops, SparseCore 0:
  10.3 41.9 all-gather.10
  54.7 37.2 all-gather.12
  94.3 37.3 all-gather.14
  133.8 37.1 all-gather.16
  173.2 52.1 all-gather.18
  227.6 51.7 all-gather.20
  2032.8 53.9 reduce-scatter.19
  2092.6 101.4 reduce-scatter.17
  2200.9 98.2 reduce-scatter.29
  2304.9 97.9 reduce-scatter.27
  2409.6 98.0 reduce-scatter.25
  2514.1 134.6 reduce-scatter.21
  2656.2 134.6 reduce-scatter.23
where the time goes:
time: 2820 us; the launch traced here: 2800 us
  local copies, waits for them, and re-layouts  1150 us (41%)
  matrix products  647 us (23%)
  waiting for transfers between devices  538 us (19%)
  blocking collectives  203 us (7%)
  other arithmetic  167 us (6%)
  starting transfers between devices  62.7 us (2%)
    dot_general x97, matrix products, inner_rows(): lax.dot_general(left, right, (((1,), (1,)), ((), ())), preferred_element_...  295 us
    reshape x36, local copies, waits for them, and re-layouts, skew_rows(): return picked.reshape(row_count, span_width - 1)[:, :key_count]  227 us
    unnamed x16, waiting for transfers between devices  215 us
    reshape x36, local copies, waits for them, and re-layouts, skew_rows(): flat_table = table_in.reshape(row_count * span_width)  193 us
    slice x36, local copies, waits for them, and re-layouts, skew_rows(): flat_table[row_count - 1:row_count - 1 + row_count * (span_width - 1)]  155 us
    reduce_scatter x1, waiting for transfers between devices, shards(): lax.psum_scatter(grad_w_outer, ('seq', 'fsdp'), scatter_dimension=0, tile...  142 us
    reduce_scatter x1, waiting for transfers between devices, shards(): lax.psum_scatter(grad_w_inner, ('seq', 'fsdp'), scatter_dimension=0, tile...  141 us
    dot_general x64, matrix products, product(): return jnp.dot(left, right, preferred_element_type=jnp.float32)  139 us
  transfers between devices with their start and end apart: 29, of which 11 were waited for; matrix products, arithmetic and copies ran while one was open for 28% of the time, Pallas kernels for 0%

commit v1 on v0

v1 whole, which is shorter than its diff:
```python
import jax
import jax.numpy as jnp
from jax import lax
from jax.experimental import pallas as pl
from jax.experimental.pallas import tpu as pltpu
from jax.sharding import PartitionSpec as P

DH = 64
BLOCK = 256
NBLK = 4
MEM = 384
L = 1024
LANES = 128

QROW = L
MROW = L + BLOCK
ROWS = L + BLOCK + MEM
KEYS = MEM + L
SPAN_M = MEM + BLOCK
SPAN_T = 2 * BLOCK
REL_M = L - BLOCK
REL_T = MEM + L - BLOCK
REL_ROWS = MEM + 2 * L

EPSILON = 1e-05
NEGATIVE = -1e30
SCORE_SCALE = 0.125
EXP2_SCALE = SCORE_SCALE * 1.4426950408889634
STEPS = NBLK + 1
BF = jnp.bfloat16
F32 = jnp.float32


def product(left, right):
    return jnp.dot(left, right, preferred_element_type=F32)


def inner_rows(left, right):
    return lax.dot_general(left, right, (((1,), (1,)), ((), ())), preferred_element_type=F32)


def inner_cols(left, right):
    return lax.dot_general(left, right, (((0,), (0,)), ((), ())), preferred_element_type=F32)


def layer_norm(values, gain, shift):
    center = values - jnp.mean(values, -1, keepdims=True)
    spread = jnp.mean(center * center, -1, keepdims=True)
    return center * lax.rsqrt(spread + EPSILON) * gain + shift


def gelu_tanh(values):
    return (
        0.5
        * values
        * (1.0 + jnp.tanh(0.7978845608028654 * (values + 0.044715 * values * values * values)))
    )


def sinusoid(row_count, width_all, farthest):
    distance = farthest - jnp.arange(row_count).astype(F32)
    frequency = 10000.0 ** (-jnp.arange(0, width_all, 2).astype(F32) / width_all)
    angles = distance[:, None] * frequency[None, :]
    return jnp.concatenate([jnp.sin(angles), jnp.cos(angles)], 1)


def split_low(values):
    high = values.astype(BF).astype(F32)
    return high, values - high


def place(step, order_ref):
    last = jnp.minimum(step, NBLK - 1)
    block = order_ref[last]
    row = jnp.where(step < NBLK, block, NBLK) * BLOCK
    return block, pl.multiple_of(row, BLOCK), last


def row_terms(q_ref, kx_ref, par_ref, row):
    query = q_ref[pl.ds(row, BLOCK), :].astype(F32)
    marks = kx_ref[pl.ds(row, BLOCK), :].astype(F32)
    return query + par_ref[0:1, :], query + par_ref[1:2, :], query + par_ref[2:3, :], marks


def forward_kernel(
    order_ref,
    q_ref,
    k_ref,
    v_ref,
    rel_ref,
    kx_ref,
    par_ref,
    att_ref,
    exp_ref,
    inv_ref,
    kcat_ref,
    vcat_ref,
    score_ref,
    lhs_ref,
    qr_ref,
):
    step = pl.program_id(1)

    @pl.when(step == 0)
    def _():
        kcat_ref[:, :LANES] = k_ref[...]
        kcat_ref[:, LANES:] = kx_ref[...]
        vcat_ref[:, :LANES] = v_ref[...]
        vcat_ref[:, LANES:] = jnp.ones((ROWS, LANES), BF)

    block, row, last = place(step, order_ref)
    lane = lax.broadcasted_iota(jnp.int32, (BLOCK, LANES), 1)
    query_w, query_r, query_s, marks = row_terms(q_ref, kx_ref, par_ref, row)
    same, other = query_s * par_ref[3:4, :], query_s * par_ref[4:5, :]
    for head in range(2):
        mine = (lane < DH) == (head == 0)
        other_sum = jnp.sum(jnp.where(mine, other, 0.0), -1, keepdims=True)
        diff = jnp.sum(jnp.where(mine, same, 0.0), -1, keepdims=True) - other_sum
        diff_high, diff_low = split_low(diff)
        other_high, other_low = split_low(other_sum)
        extra = jnp.where(lane < 3, marks * diff_high, jnp.where(lane < 6, marks * diff_low, 0.0))
        extra = jnp.where(lane == 6, other_high, jnp.where(lane == 7, other_low, extra))
        extra = jnp.where(lane == 8, NEGATIVE, extra)
        lhs_ref[head, :, :LANES] = jnp.where(mine, query_w, 0.0).astype(BF)
        lhs_ref[head, :, LANES:] = extra.astype(BF)
        qr_ref[head] = jnp.where(mine, query_r, 0.0).astype(BF)

    def scores(head, key_row, key_count, rel_row):
        content = inner_rows(lhs_ref[head], kcat_ref[pl.ds(key_row, key_count), :])
        span = key_count + BLOCK
        position = inner_rows(qr_ref[head], rel_ref[pl.ds(rel_row, span), :])
        position = pltpu.roll(position, span - BLOCK + 1, 1, stride=1, stride_axis=0)
        return content + position[:, :key_count]

    def widest(running, tile):
        for at in range(0, tile.shape[1], LANES):
            piece = tile[:, at : at + LANES]
            running = piece if running is None else jnp.maximum(running, piece)
        return running

    tops = []
    rel_row = pl.multiple_of(REL_M - BLOCK * block, BLOCK)
    for head in range(2):
        tile = scores(head, MROW, MEM, rel_row)
        score_ref[head, :, :MEM] = tile
        tops.append(widest(None, tile))

    def column(at):
        return pl.multiple_of(MEM + BLOCK * at, LANES)

    def token_tile(at, tops):
        key_block = order_ref[at]
        key_row = pl.multiple_of(BLOCK * key_block, BLOCK)
        rel_row = pl.multiple_of(REL_T + BLOCK * (key_block - block), LANES)
        fresh = []
        for head in range(2):
            tile = scores(head, key_row, BLOCK, rel_row)
            score_ref[head, :, pl.ds(column(at), BLOCK)] = tile
            fresh.append(widest(tops[head], tile))
        return tuple(fresh)

    tops = lax.fori_loop(0, last, token_tile, tuple(tops))
    across = lax.broadcasted_iota(jnp.int32, (BLOCK, BLOCK), 0) - lax.broadcasted_iota(
        jnp.int32, (BLOCK, BLOCK), 1
    )
    hidden_at = jnp.where(step < NBLK, BLOCK, 0)
    own_row = pl.multiple_of(BLOCK * block, BLOCK)
    peaks = []
    for head in range(2):
        tile = scores(head, own_row, BLOCK, REL_T)
        tile = jnp.where(across == hidden_at, NEGATIVE, tile)
        score_ref[head, :, pl.ds(column(last), BLOCK)] = tile
        peaks.append(jnp.max(widest(tops[head], tile), -1, keepdims=True))

    def weigh(head, at, key_row, key_count):
        tile = score_ref[head, :, pl.ds(at, key_count)]
        low = jnp.exp2((tile - peaks[head]) * EXP2_SCALE).astype(BF)
        exp_ref[head, :, pl.ds(at, key_count)] = low
        return product(low, vcat_ref[pl.ds(key_row, key_count), :])

    sums = tuple(weigh(head, 0, MROW, MEM) for head in range(2))

    def token_sum(at, sums):
        key_row = pl.multiple_of(BLOCK * order_ref[at], BLOCK)
        return tuple(sums[head] + weigh(head, column(at), key_row, BLOCK) for head in range(2))

    sums = lax.fori_loop(0, last + 1, token_sum, sums)
    first = lane < DH
    inverse = 1.0 / jnp.where(first, sums[0][:, LANES:], sums[1][:, LANES:])
    total = jnp.where(first, sums[0][:, :LANES], sums[1][:, :LANES])
    att_ref[pl.ds(row, BLOCK), :] = (total * inverse).astype(BF)
    inv_ref[pl.ds(row, BLOCK), :] = inverse


def backward_kernel(
    order_ref,
    q_ref,
    k_ref,
    v_ref,
    rel_ref,
    kx_ref,
    par_ref,
    grad_ref,
    att_ref,
    inv_ref,
    exp_ref,
    dq_ref,
    dk_ref,
    dv_ref,
    drel_ref,
    dpar_ref,
    kcat_ref,
    vcat_ref,
    flip_ref,
    lhs_ref,
    qwt_ref,
    qrt_ref,
    gt_ref,
    dkt_ref,
    dvt_ref,
    drelt_ref,
    accw_ref,
    accr_ref,
):
    step = pl.program_id(1)

    @pl.when(step == 0)
    def _():
        kcat_ref[:, :LANES] = k_ref[...]
        kcat_ref[:, LANES:] = kx_ref[...]
        vcat_ref[:, :LANES] = (v_ref[...].astype(F32) * SCORE_SCALE).astype(BF)
        vcat_ref[:, LANES:] = jnp.full((ROWS, LANES), SCORE_SCALE, BF)
        up = lax.broadcasted_iota(jnp.int32, (BLOCK, BLOCK), 0)
        down = lax.broadcasted_iota(jnp.int32, (BLOCK, BLOCK), 1)
        flip_ref[...] = jnp.where(up + down == BLOCK - 1, 1.0, 0.0).astype(BF)
        dkt_ref[...] = jnp.zeros_like(dkt_ref)
        dvt_ref[...] = jnp.zeros_like(dvt_ref)
        drelt_ref[...] = jnp.zeros_like(drelt_ref)
        dpar_ref[...] = jnp.zeros_like(dpar_ref)

    block, row, last = place(step, order_ref)
    lane = lax.broadcasted_iota(jnp.int32, (BLOCK, LANES), 1)
    query_w, query_r, query_s, marks = row_terms(q_ref, kx_ref, par_ref, row)
    grad_low = (grad_ref[pl.ds(row, BLOCK), :].astype(F32) * inv_ref[pl.ds(row, BLOCK), :]).astype(
        BF
    )
    grad = grad_low.astype(F32)
    dots = grad * att_ref[pl.ds(row, BLOCK), :].astype(F32)
    for head in range(2):
        mine = (lane < DH) == (head == 0)
        high, low = split_low(-jnp.sum(jnp.where(mine, dots, 0.0), -1, keepdims=True))
        extra = jnp.where(lane == 0, high, jnp.where(lane == 1, low, 0.0))
        lhs_ref[head, :, :LANES] = jnp.where(mine, grad, 0.0).astype(BF)
        lhs_ref[head, :, LANES:] = extra.astype(BF)
    flip = flip_ref[...]
    qwt_ref[...] = query_w.astype(BF).astype(F32).T.astype(BF)
    qrt_ref[...] = product(flip, query_r.astype(BF)).T.astype(BF)
    gt_ref[...] = grad.T.astype(BF)
    accw_ref[...] = jnp.zeros_like(accw_ref)
    accr_ref[...] = jnp.zeros_like(accr_ref)

    def tile(head, at, key_row, key_count, rel_row):
        span = key_count + BLOCK
        own = slice(DH * head, DH * head + DH)
        keys = pl.ds(key_row, key_count)
        span_at = pl.ds(rel_row, span)
        probs = exp_ref[head, :, pl.ds(at, key_count)]
        slope = inner_rows(lhs_ref[head], vcat_ref[keys, :])
        scaled = (probs.astype(F32) * slope).astype(BF)
        accw_ref[head] += product(scaled, kcat_ref[keys, :])
        dkt_ref[own, keys] += product(qwt_ref[own, :], scaled)
        dvt_ref[own, keys] += product(gt_ref[own, :], probs)
        turned = product(flip, scaled).astype(BF)
        turned = jnp.concatenate([turned, jnp.zeros((BLOCK, BLOCK), BF)], 1)
        turned = pltpu.roll(turned, 0, 1, stride=1, stride_axis=0)
        accr_ref[head] += product(turned, rel_ref[span_at, :])
        drelt_ref[own, span_at] += product(qrt_ref[own, :], turned)

    rel_row = pl.multiple_of(REL_M - BLOCK * block, BLOCK)
    for head in range(2):
        tile(head, 0, MROW, MEM, rel_row)

    def token_tile(at, carry):
        key_block = order_ref[at]
        key_row = pl.multiple_of(BLOCK * key_block, BLOCK)
        rel_row = pl.multiple_of(REL_T + BLOCK * (key_block - block), LANES)
        for head in range(2):
            tile(head, pl.multiple_of(MEM + BLOCK * at, LANES), key_row, BLOCK, rel_row)
        return carry

    lax.fori_loop(0, last + 1, token_tile, 0)

    first = lane < DH
    grad_w = jnp.where(first, accw_ref[0, :, :LANES], accw_ref[1, :, :LANES])
    high, low = split_low(jnp.where(first, accr_ref[0], accr_ref[1]))
    grad_r = product(flip, high.astype(BF)) + product(flip, low.astype(BF))
    same_sums, other_sums = [], []
    for head in range(2):
        sums = accw_ref[head, :, LANES:]
        same_sums.append(jnp.sum(jnp.where(lane < 3, marks * sums, 0.0), -1, keepdims=True))
        total = jnp.sum(jnp.where(lane == 6, sums, 0.0), -1, keepdims=True)
        other_sums.append(total - same_sums[head])
    same = jnp.where(first, same_sums[0], same_sums[1])
    other = jnp.where(first, other_sums[0], other_sums[1])
    grad_s = same * par_ref[3:4, :] + other * par_ref[4:5, :]
    dq_ref[pl.ds(row, BLOCK), :] = (grad_w + grad_r + grad_s).astype(BF)
    for at, rows in enumerate((grad_w, grad_r, grad_s, same * query_s, other * query_s)):
        dpar_ref[at : at + 1, :] += jnp.sum(rows, 0, keepdims=True)

    @pl.when(step == STEPS - 1)
    def _():
        dk_ref[...] = dkt_ref[...].T.astype(BF)
        dv_ref[...] = dvt_ref[...].T.astype(BF)
        drel_ref[...] = drelt_ref[...].T.astype(BF)


def attention_specs(pairs):
    def column(rows, first):
        return pl.BlockSpec((rows, LANES), lambda pair, step, order: (0, first + pair))

    shared = pl.BlockSpec((ROWS, LANES), lambda pair, step, order: (0, 0))
    ins = [
        column(ROWS, 0),
        column(ROWS, pairs),
        column(ROWS, 2 * pairs),
        column(REL_ROWS, 0),
        shared,
        column(8, 0),
    ]
    exps = pl.BlockSpec(
        (None, None, 2, BLOCK, KEYS), lambda pair, step, order: (pair, step, 0, 0, 0)
    )
    return column, ins, exps


PARAMS = dict(
    dimension_semantics=("arbitrary", "arbitrary"), vmem_limit_bytes=48 * 1024 * 1024
)


def attention_forward(order, qkv, rel, marks, par):
    pairs = rel.shape[1] // LANES
    column, ins, exps = attention_specs(pairs)
    width = pairs * LANES
    return pl.pallas_call(
        forward_kernel,
        grid_spec=pltpu.PrefetchScalarGridSpec(
            num_scalar_prefetch=1,
            grid=(pairs, STEPS),
            in_specs=ins,
            out_specs=[column(MROW, 0), exps, column(MROW, 0)],
            scratch_shapes=[
                pltpu.VMEM((ROWS, 2 * LANES), BF),
                pltpu.VMEM((ROWS, 2 * LANES), BF),
                pltpu.VMEM((2, BLOCK, KEYS), F32),
                pltpu.VMEM((2, BLOCK, 2 * LANES), BF),
                pltpu.VMEM((2, BLOCK, LANES), BF),
            ],
        ),
        out_shape=[
            jax.ShapeDtypeStruct((MROW, width), BF),
            jax.ShapeDtypeStruct((pairs, STEPS, 2, BLOCK, KEYS), BF),
            jax.ShapeDtypeStruct((MROW, width), F32),
        ],
        compiler_params=pltpu.CompilerParams(**PARAMS),
    )(order, qkv, qkv, qkv, rel, marks, par)


def attention_backward(order, qkv, rel, marks, par, grad, att, inverse, exps_in):
    pairs = rel.shape[1] // LANES
    column, ins, exps = attention_specs(pairs)
    width = pairs * LANES
    return pl.pallas_call(
        backward_kernel,
        grid_spec=pltpu.PrefetchScalarGridSpec(
            num_scalar_prefetch=1,
            grid=(pairs, STEPS),
            in_specs=ins + [column(MROW, 0)] * 3 + [exps],
            out_specs=[
                column(MROW, 0),
                column(ROWS, 0),
                column(ROWS, 0),
                column(REL_ROWS, 0),
                column(8, 0),
            ],
            scratch_shapes=[
                pltpu.VMEM((ROWS, 2 * LANES), BF),
                pltpu.VMEM((ROWS, 2 * LANES), BF),
                pltpu.VMEM((BLOCK, BLOCK), BF),
                pltpu.VMEM((2, BLOCK, 2 * LANES), BF),
                pltpu.VMEM((LANES, BLOCK), BF),
                pltpu.VMEM((LANES, BLOCK), BF),
                pltpu.VMEM((LANES, BLOCK), BF),
                pltpu.VMEM((LANES, ROWS), F32),
                pltpu.VMEM((LANES, ROWS), F32),
                pltpu.VMEM((LANES, REL_ROWS), F32),
                pltpu.VMEM((2, BLOCK, 2 * LANES), F32),
                pltpu.VMEM((2, BLOCK, LANES), F32),
            ],
        ),
        out_shape=[
            jax.ShapeDtypeStruct((MROW, width), BF),
            jax.ShapeDtypeStruct((ROWS, width), BF),
            jax.ShapeDtypeStruct((ROWS, width), BF),
            jax.ShapeDtypeStruct((REL_ROWS, width), BF),
            jax.ShapeDtypeStruct((8, width), F32),
        ],
        compiler_params=pltpu.CompilerParams(**PARAMS),
    )(order, qkv, qkv, qkv, rel, marks, par, grad, att, inverse, exps_in)


def swap(values):
    return lax.ppermute(values, "seq", [(0, 1), (1, 0)])


def pad_to(values, count):
    return jnp.pad(values, (0, count - values.shape[0]))


def shards(
    hidden,
    query_in,
    memory,
    segment_ids,
    block_order,
    memory_valid,
    w_query,
    w_key,
    w_value,
    w_out,
    w_rel,
    rel_biases,
    seg_embed,
    w_inner,
    b_inner,
    w_outer,
    b_outer,
    norm_gains,
    norm_biases,
    grad_hidden_out,
    grad_query_out,
):
    side = lax.axis_index("seq")
    groups = lax.axis_size("fsdp")
    half, width = hidden.shape[1:]
    target_half = query_in.shape[1]
    memory_half = memory.shape[1]
    head_width = w_rel.shape[1]
    shard_rows = w_query.shape[0]
    ffn_width = w_inner.shape[1]
    own_rows = half + target_half

    def own_columns(weight):
        return lax.dynamic_slice_in_dim(weight, side * head_width, head_width, 1)

    smalls = (rel_biases, seg_embed, b_inner, b_outer, norm_gains, norm_biases)
    small_flat = pad_to(jnp.concatenate([s.reshape(-1) for s in smalls]), shard_rows * LANES)
    packed = jnp.concatenate(
        [
            own_columns(w_query),
            own_columns(w_key),
            own_columns(w_value),
            w_rel,
            small_flat.reshape(shard_rows, LANES),
        ],
        1,
    )
    packed = lax.all_gather(packed, "fsdp", axis=0, tiled=True)
    mixed = lax.all_gather(
        jnp.concatenate([w_out, w_inner], 1), "fsdp", axis=0, tiled=True
    )
    full_outer = lax.all_gather(w_outer, "fsdp", axis=0, tiled=True)
    full_out, full_inner = mixed[:, :width], mixed[:, width:]
    head_weights = packed[:, : 3 * head_width]
    rel_weight = packed[:, 3 * head_width : 4 * head_width]
    small_all = packed[:, 4 * head_width :].reshape(groups, shard_rows * LANES).astype(F32)

    def unpack():
        found, at = [], 0
        for small in smalls:
            piece = small_all[:, at : at + small.size].reshape((groups,) + small.shape)
            found.append(jnp.moveaxis(piece, 0, -2).reshape(small.shape[:-1] + (-1,)))
            at += small.size
        return found

    all_biases, all_seg, inner_bias, outer_bias, gains, shifts = unpack()

    mine = jnp.concatenate([hidden[0], query_in[0], memory[0]], 0)
    theirs = swap(mine)
    low = jnp.where(side == 0, mine, theirs)
    high = jnp.where(side == 0, theirs, mine)
    cuts = ((0, half), (half, own_rows), (own_rows, own_rows + memory_half))
    stacked = jnp.concatenate([part[a:b] for a, b in cuts for part in (low, high)], 0)

    qkv = product(stacked, head_weights).astype(BF)
    pos_table = sinusoid(REL_ROWS, width, MEM + L - 1).astype(BF)
    rel = product(pos_table, rel_weight).astype(BF)
    par = jnp.concatenate([all_biases, all_seg, jnp.zeros((3, head_width), F32)], 0)
    order = block_order[0]
    segs = segment_ids[0]
    target_seg = lax.dynamic_slice_in_dim(segs, MEM + order[NBLK - 1] * BLOCK, BLOCK)
    seg_rows = jnp.concatenate([segs[MEM:], target_seg, segs[:MEM]])
    invalid = jnp.concatenate([jnp.zeros((MROW,), jnp.int32), (memory_valid[0] != 1).astype(jnp.int32)])
    lane = jnp.arange(LANES)[None, :]
    marks = jnp.where(lane < 6, seg_rows[:, None] == lane % 3, (lane == 6) | (lane == 7))
    marks = jnp.where(lane == 8, invalid[:, None] == 1, marks).astype(BF)

    att, exps, inverse = attention_forward(order, qkv, rel, marks, par)

    def rows_of(values, which):
        return jnp.concatenate(
            [
                lax.dynamic_slice_in_dim(values, which * half, half, 0),
                lax.dynamic_slice_in_dim(values, L + which * target_half, target_half, 0),
            ],
            0,
        )

    def by_side(own, other, axis):
        return jnp.where(
            side == 0,
            jnp.concatenate([own, other], axis),
            jnp.concatenate([other, own], axis),
        )

    attn_rows = by_side(rows_of(att, side), swap(rows_of(att, 1 - side)), 1)
    first_sum = product(attn_rows, full_out) + mine[:own_rows].astype(F32)
    first_norm = layer_norm(first_sum, gains[0], shifts[0])
    first_low = first_norm.astype(BF)
    hidden_pre = product(first_low, full_inner) + inner_bias
    activation = gelu_tanh(hidden_pre).astype(BF)
    second_sum = product(activation, full_outer) + outer_bias + first_norm
    result = layer_norm(second_sum, gains[1], shifts[1]).astype(BF)
    grad_rows = jnp.concatenate([grad_hidden_out[0], grad_query_out[0]], 0).astype(F32)
    second_pull = jax.vjp(layer_norm, second_sum, gains[1], shifts[1])[1]
    grad_second, grad_gain_two, grad_shift_two = second_pull(grad_rows)
    grad_outer_low = grad_second.astype(BF)
    grad_b_outer = jnp.sum(grad_outer_low.astype(F32), 0)
    grad_w_outer = inner_cols(activation, grad_outer_low)
    gelu_pull = jax.vjp(gelu_tanh, hidden_pre)[1]
    grad_pre = gelu_pull(inner_rows(grad_outer_low, full_outer))[0].astype(BF)
    grad_b_inner = jnp.sum(grad_pre.astype(F32), 0)
    grad_w_inner = inner_cols(first_low, grad_pre)
    grad_first = grad_second + inner_rows(grad_pre, full_inner)
    first_pull = jax.vjp(layer_norm, first_sum, gains[0], shifts[0])[1]
    grad_sum_one, grad_gain_one, grad_shift_one = first_pull(grad_first)
    grad_mixed = grad_sum_one.astype(BF)
    grad_w_out = inner_cols(attn_rows, grad_mixed)
    grad_attn = inner_rows(grad_mixed, full_out).astype(BF)

    devices = 2 * groups
    out_rows = width // devices
    token_smalls = (
        grad_b_inner.reshape(devices, -1),
        grad_b_outer.reshape(devices, -1),
        jnp.stack([grad_gain_one, grad_gain_two]).reshape(2, devices, -1),
        jnp.stack([grad_shift_one, grad_shift_two]).reshape(2, devices, -1),
    )
    token_flat = jnp.concatenate(
        [s if s.ndim == 2 else s.transpose(1, 0, 2).reshape(devices, -1) for s in token_smalls], 1
    )
    token_count = token_flat.shape[1]
    token_flat = jnp.pad(token_flat, ((0, 0), (0, out_rows * LANES - token_count)))
    token_packed = jnp.concatenate(
        [grad_w_out, grad_w_inner, token_flat.reshape(width, LANES)], 1
    ).astype(BF)
    everywhere = ("seq", "fsdp")
    token_sums = lax.psum_scatter(token_packed, everywhere, scatter_dimension=0, tiled=True)
    out_outer = lax.psum_scatter(
        grad_w_outer.astype(BF), everywhere, scatter_dimension=0, tiled=True
    ).astype(F32)
    token_sums = token_sums.astype(F32)
    out_out = token_sums[:, :width]
    out_inner = token_sums[:, width : width + ffn_width]
    small_sums = token_sums[:, width + ffn_width :].reshape(-1)
    inner_count, row_count = ffn_width // devices, width // devices
    out_b_inner = small_sums[:inner_count]
    at = inner_count
    out_b_outer = small_sums[at : at + row_count]
    at += row_count
    out_gains = small_sums[at : at + 2 * row_count].reshape(2, row_count)
    at += 2 * row_count
    out_shifts = small_sums[at : at + 2 * row_count].reshape(2, row_count)

    own_grad = lax.dynamic_slice_in_dim(grad_attn, side * head_width, head_width, 1)
    far_grad = swap(lax.dynamic_slice_in_dim(grad_attn, (1 - side) * head_width, head_width, 1))
    head_grad = jnp.concatenate(
        [by_side(own_grad[a:b], far_grad[a:b], 0) for a, b in cuts[:2]], 0
    )
    dq, dk, dv, drel, dpar = attention_backward(
        order, qkv, rel, marks, par, head_grad, att, inverse, exps
    )

    weight_q = head_weights[:, :head_width]
    weight_k = head_weights[:, head_width : 2 * head_width]
    weight_v = head_weights[:, 2 * head_width :]

    def back_rows(which):
        return (
            inner_rows(rows_of(dq, which), weight_q)
            + jnp.pad(
                inner_rows(
                    lax.dynamic_slice_in_dim(dk, which * half, half, 0), weight_k
                )
                + inner_rows(
                    lax.dynamic_slice_in_dim(dv, which * half, half, 0), weight_v
                ),
                ((0, target_half), (0, 0)),
            )
        )

    far_rows = swap(back_rows(1 - side).astype(BF)).astype(F32)
    grad_own = grad_sum_one + back_rows(side) + far_rows

    grad_head = jnp.concatenate(
        [inner_cols(stacked[:MROW], dq), inner_cols(stacked, dk), inner_cols(stacked, dv)], 1
    ).astype(BF)
    grad_head = grad_head.reshape(2, groups, out_rows, 3 * head_width)
    grad_head = grad_head.transpose(1, 0, 2, 3).reshape(width, 3 * head_width)
    grad_rel = inner_cols(pos_table, drel).astype(BF)
    bias_count = head_width // groups
    head_flat = dpar[:5].reshape(5, groups, bias_count).transpose(1, 0, 2).reshape(groups, -1)
    head_flat = jnp.pad(head_flat, ((0, 0), (0, shard_rows * LANES - 5 * bias_count)))
    head_packed = jnp.concatenate(
        [grad_head, grad_rel, head_flat.reshape(width, LANES).astype(BF)], 1
    )
    head_sums = lax.psum_scatter(head_packed, "fsdp", scatter_dimension=0, tiled=True)
    own_sum = lax.dynamic_slice_in_dim(head_sums, side * out_rows, out_rows, 0)
    far_sum = lax.dynamic_slice_in_dim(head_sums, (1 - side) * out_rows, out_rows, 0)
    own_sum = own_sum[:, : 3 * head_width].astype(F32)
    far_sum = swap(far_sum[:, : 3 * head_width]).astype(F32)
    out_query, out_key, out_value = (
        by_side(
            own_sum[:, at * head_width : (at + 1) * head_width],
            far_sum[:, at * head_width : (at + 1) * head_width],
            1,
        )
        for at in range(3)
    )
    out_rel = head_sums[:, 3 * head_width : 4 * head_width].astype(F32)
    small_head = head_sums[:, 4 * head_width :].reshape(-1).astype(F32)
    out_biases = small_head[: 3 * bias_count].reshape(3, bias_count)
    out_seg = small_head[3 * bias_count : 5 * bias_count].reshape(2, bias_count)
    return (
        result[None, :half],
        result[None, half:],
        grad_own[None, :half],
        grad_own[None, half:],
        out_query,
        out_key,
        out_value,
        out_out,
        out_rel,
        out_biases,
        out_seg,
        out_inner,
        out_b_inner,
        out_outer,
        out_b_outer,
        out_gains,
        out_shifts,
    )


def solution(mesh):
    rows = P("fsdp", "seq", None)
    both = ("seq", "fsdp")
    in_specs = (
        (rows,) * 3
        + (P("fsdp", None),) * 7
        + (P("fsdp", "seq"), P(None, both), P(None, both))
        + (P("fsdp", None), P("fsdp"), P("fsdp", None), P("fsdp"))
        + (P(None, "fsdp"), P(None, "fsdp"))
        + (rows,) * 2
    )
    out_specs = (
        (rows,) * 4
        + (P(both, None),) * 4
        + (P("fsdp", "seq"), P(None, both), P(None, both))
        + (P(both, None), P(both), P(both, None), P(both))
        + (P(None, both), P(None, both))
    )
    return jax.shard_map(shards, mesh=mesh, in_specs=in_specs, out_specs=out_specs, check_vma=False)
```

time: 2820 us -> 651 us (0.23)
  local copies, waits for them, and re-layouts: 1150 us -> 55.5 us
  matrix products: 647 us -> 89.3 us
  waiting for transfers between devices: 538 us -> 281 us
  blocking collectives: 203 us -> 0 us
  Pallas kernels: 0 us -> 142 us
  other arithmetic: 167 us -> 47.1 us
  starting transfers between devices: 62.7 us -> 9.46 us
    reshape x129 -> x19, local copies, waits for them, and re-layouts: 640 us -> 9.77 us  [the longest x4 3.07 us: shards(): s.reshape(-1)]
    dot_general x97 -> x9, matrix products: 295 us -> 23.6 us  [inner_rows(): lax.dot_general(left, right, (((1,), (1,)), ((), ())), preferred_element_...]
    dot_general x137 -> x5, matrix products: 233 us -> 30.9 us  [product(): return jnp.dot(left, right, preferred_element_type=F32)]
    reduce_scatter x4 -> x2, waiting for transfers between devices: 283 us -> 92.7 us  [the longest x1 92.7 us: shards(): lax.psum_scatter(grad_w_outer.astype(BF), everywhere, scatter_dimension=0...]
    slice x90 -> x29, local copies, waits for them, and re-layouts: 180 us -> 16.5 us  [the longest x4 4.04 us: shards(): part[a:b]]
    pallas_call x0 -> x2, Pallas kernels: none -> 142 us  [the longest x1 88.2 us: attention_backward(): pl.pallas_call(backward_kernel, grid_spec=pltpu.PrefetchScalarGridSpec(nu...]
    unnamed x3 -> x0, blocking collectives: 104 us -> none
    unnamed x16 -> x7, waiting for transfers between devices: 215 us -> 115 us
  transfers between devices with their start and end apart: 29 -> 11, of which waited for: 11 -> 8; matrix products, arithmetic and copies ran while one was open for 28% -> 18% of each run, Pallas kernels for 0% -> 8%
where the time goes in v1:
time: 651 us; the launch traced here: 640 us
  waiting for transfers between devices  281 us (43%)
  Pallas kernels  142 us (22%)
  matrix products  89.3 us (14%)
  local copies, waits for them, and re-layouts  55.5 us (9%)
  other arithmetic  47.1 us (7%)
  between operations  16.1 us (2%)
  starting transfers between devices  9.46 us (1%)
    unnamed x7, waiting for transfers between devices  115 us
    reduce_scatter x1, waiting for transfers between devices, shards(): lax.psum_scatter(grad_w_outer.astype(BF), everywhere, scatter_dimension=0...  92.7 us
    pallas_call x1, Pallas kernels, attention_backward(): pl.pallas_call(backward_kernel, grid_spec=pltpu.PrefetchScalarGridSpec(nu...  88.2 us
    pallas_call x1, Pallas kernels, attention_forward(): pl.pallas_call(forward_kernel, grid_spec=pltpu.PrefetchScalarGridSpec(num...  53.6 us
    ppermute x5, waiting for transfers between devices, swap(): return lax.ppermute(values, 'seq', [(0, 1), (1, 0)])  50.8 us
    dot_general x7, matrix products, inner_cols(): lax.dot_general(left, right, (((0,), (0,)), ((), ())), preferred_element_...  34.8 us
    dot_general x5, matrix products, product(): return jnp.dot(left, right, preferred_element_type=F32)  30.9 us
    dot_general x9, matrix products, inner_rows(): lax.dot_general(left, right, (((1,), (1,)), ((), ())), preferred_element_...  23.6 us
  transfers between devices with their start and end apart: 11, of which 8 were waited for; matrix products, arithmetic and copies ran while one was open for 18% of the time, Pallas kernels for 8%

profile of v1, /device:TPU:0, one launch (start us, length us, event | category | flops | bytes accessed | tf_op | source)
XLA Modules:
  0.0 640.5 jit_solution(3270881905888547687)
XLA Ops:
  13.5 1.4 concatenate.118
  15.7 1.8 pad_maximum_fusion.11
  18.3 1.1 pad_maximum_fusion.7
  19.4 3.0 collective-permute-start
  23.9 1.1 select_convert_fusion.kx_ref
  25.1 15.7 %fusion.10 = (bf16[2432,384]{1,0:T(8,128)(2,1)S(1)}, bf16[2432,384]{1,0:T(8,128)(2,1)}) fusion(f32[384]{0:T(512)S(1)} %multiply_power_fusion, f32[2432]{0:T(1024)S(1)} %convert_subtract_fusion), kind=kLoop, calls=%fused_computation.22 | loop fusion | flops 2801664 | bytes 3746816 | tf_op jit(solution)/shard_map/convert.41
  40.8 10.0 %collective-permute-done = bf16[832,768]{1,0:T(8,128)(2,1)} collective-permute-done((bf16[832,768]{1,0:T(8,128)(2,1)}, bf16[832,768]{1,0:T(8,128)(2,1)}, u32[]{:S(2)}, u32[]{:S(2)}) %collective-permute-start) | collective-permute-done | bytes 1277984 | tf_op jit(solution)/shard_map/ppermute | solution.py:413
  50.8 1.8 broadcast_select_fusion
  52.6 1.3 fusion.79
  53.8 1.2 fusion.80
  58.1 3.3 all-gather.4.cloned.1.call-done
  61.4 1.0 slice_convert_fusion
  65.1 3.9 convolution_convert_fusion.3.rel_ref
  69.0 7.8 %convolution_convert_fusion.q_ref.k_ref.v_ref = bf16[1664,1152]{1,0:T(8,128)(2,1)} fusion(bf16[1664,768]{1,0:T(8,128)(2,1)} %slice_dynamic-update-slice_fusion, bf16[768,1664]{1,0:T(8,128)(2,1)S(1)} %copy-done.12), kind=kOutput, calls=%fused_computation.11 | convolution fusion | flops 2946318336 | bytes 8159232 | tf_op jit(solution)/shard_map/dot_general | solution.py:35
  76.9 53.6 %shard_map.332 = (bf16[1280,384]{1,0:T(8,128)(2,1)S(1)}, bf16[3,5,2,256,1408]{4,3,2,1,0:T(8,128)(2,1)}, f32[1280,384]{1,0:T(8,128)S(1)}) custom-call(s32[4]{0:T(128)S(1)} %bitcast.54, bf16[1664,1152]{1,0:T(8,128)(2,1)} %convolution_convert_fusion.q_ref.k_ref.v_ref, bf16[1664,1152]{1,0:T(8,128)(2,1)} %convolution_convert_fusion.q_ref.k_ref.v_ref, ...), custom_call_target="tpu_custom_call" | custom-call | tf_op jit(solution)/shard_map/pallas_call | solution.py:345
  130.5 1.3 copy-done.1
  132.8 1.4 collective-permute-start.1
  136.6 9.9 %collective-permute-done.1 = bf16[640,384]{1,0:T(8,128)(2,1)} collective-permute-done((bf16[640,384]{1,0:T(8,128)(2,1)}, bf16[640,384]{1,0:T(8,128)(2,1)}, u32[]{:S(2)}, u32[]{:S(2)}) %collective-permute-start.1) | collective-permute-done | bytes 491552 | tf_op jit(solution)/shard_map/ppermute | solution.py:413
  146.5 2.7 fusion.88
  150.6 6.1 fusion.8
  156.7 19.7 %all-gather.8.cloned.1.call-done = bf16[3072,768]{1,0:T(8,128)(2,1)} async-done(((bf16[192,768]{1,0:T(8,128)(2,1)}), bf16[3072,768]{1,0:T(8,128)(2,1)}) %all-gather.8.cloned.1.call-update) | async-done | bytes 4718608 | tf_op jit(solution)/shard_map/all_gather | solution.py:472
  176.4 10.3 %fusion.89 = (f32[640]{0:T(1024)S(1)}, f32[640,768]{1,0:T(8,128)S(1)}) fusion(f32[768]{0:T(1024)S(1)} %add.204, f32[768]{0:T(1024)S(1)} %mul.260, f32[640]{0:T(1024)S(1)} %fusion.65, f32[640,768]{1,0:T(8,128)} %copy-done.9, f32[640]{0:T(1024)S(1)} %broadcast_multiply_fusion.1, f32[768]{0:T(1024)S(1)} %add.212, ...), kind=kOutput, calls=%fused_computation.194 | convolution fusion | flops 3042999808 | bytes 16544256 | tf_op jit(solution)/shard_map/dot_general | solution.py:35
  187.9 1.4 fusion.16
  189.3 1.8 fusion.78
  192.1 11.1 %fusion.74 = (bf16[3072]{0:T(1024)(128)(2,1)}, bf16[640,3072]{1,0:T(8,128)(2,1)}) fusion(f32[640,3072]{1,0:T(8,128)S(1)} %copy-done.46, f32[3072]{0:T(1024)S(1)} %add.207, bf16[640,768]{1,0:T(8,128)(2,1)S(1)} %get-tuple-element.45, bf16[3072,768]{1,0:T(8,128)(2,1)S(1)} %bitcast.86), kind=kOutput, calls=%fused_computation.180 | convolution fusion | flops 3071013888 | bytes 17516544 | tf_op jit(solution)/shard_map/dot_general | solution.py:39
  203.2 6.4 %multiply_reduce_fusion = (bf16[768]{0:T(1024)(128)(2,1)}, f32[640]{0:T(1024)S(1)}, bf16[768]{0:T(1024)(128)(2,1)S(1)}, f32[640,768]{1,0:T(8,128)S(1)}) fusion(f32[640,768]{1,0:T(8,128)S(1)} %copy-done.10, f32[640]{0:T(1024)S(1)} %fusion.65, f32[640]{0:T(1024)S(1)} %broadcast_multiply_fusion.1, f32[768]{0:T(1024)S(1)} %mul.260, ...), kind=kOutput, calls=%fused_computation.43 | convolution fusion | flops 3024811776 | bytes 14571008 | tf_op jit(solution)/shard_map/dot_general | solution.py:39
  210.4 1.0 convolution_convert_fusion.5
  212.5 1.5 collective-permute-start.2
  214.1 12.2 %collective-permute-done.2 = bf16[640,384]{1,0:T(8,128)(2,1)} collective-permute-done((bf16[640,384]{1,0:T(8,128)(2,1)}, bf16[640,384]{1,0:T(8,128)(2,1)}, u32[]{:S(2)}, u32[]{:S(2)}) %collective-permute-start.2) | collective-permute-done | bytes 491552 | tf_op jit(solution)/shard_map/ppermute | solution.py:413
  227.2 1.0 slice.273
  228.6 88.2 %shard_map.333 = (bf16[1280,384]{1,0:T(8,128)(2,1)S(1)}, bf16[1664,384]{1,0:T(8,128)(2,1)S(1)}, bf16[1664,384]{1,0:T(8,128)(2,1)S(1)}, bf16[2432,384]{1,0:T(8,128)(2,1)}, f32[8,384]{1,0:T(8,128)S(1)}) custom-call(s32[4]{0:T(128)S(1)} %bitcast.55, bf16[1664,1152]{1,0:T(8,128)(2,1)} %convolution_convert_fusion.q_ref.k_ref.v_ref, ...), custom_call_target="tpu_custom_call" | custom-call | tf_op jit(solution)/shard_map/pallas_call | solution.py:373
  316.8 1.0 copy-done.2
  317.9 1.0 copy-done.4
  319.9 4.5 fusion.32
  324.4 1.1 copy.55
  325.5 3.4 convolution_convert_fusion.6
  328.9 3.4 convolution_convert_fusion.7
  332.4 1.2 fusion.29
  334.9 1.7 pad_maximum_fusion.2
  336.7 10.8 %convolution_convert_fusion.1 = bf16[3072,768]{1,0:T(8,128)(2,1)} fusion(bf16[640,768]{1,0:T(8,128)(2,1)} %copy-done.21, f32[640,3072]{1,0:T(8,128)} %fusion.8, f32[3072]{0:T(1024)S(1)} %add.207), kind=kOutput, calls=%fused_computation.15 | convolution fusion | flops 3041918976 | bytes 13578240 | tf_op jit(solution)/shard_map/dot_general | solution.py:43
  347.9 1.3 reduce.3
  349.2 1.0 reduce.4
  353.0 1.4 copy.59
  354.3 1.4 stack.19
  355.7 1.3 stack.18
  358.5 1.4 copy.58
  361.4 1.5 fusion.60
  362.8 1.7 reshape.299
  364.5 4.4 convolution_convert_fusion.4
  369.0 2.4 copy.60
  371.5 7.0 %convolution_convert_fusion.2 = bf16[768,3072]{1,0:T(8,128)(2,1)S(1)} fusion(bf16[640,3072]{1,0:T(8,128)(2,1)} %get-tuple-element.43, f32[640,768]{1,0:T(8,128)} %copy-done.9, f32[768]{0:T(1024)S(1)} %copy-done.44, f32[768]{0:T(1024)S(1)} %copy-done.39, f32[640]{0:T(1024)S(1)} %copy-done.41, f32[640]{0:T(1024)S(1)} %copy-done.35), kind=kOutput, calls=%fused_computation.16 | convolution fusion | flops 3024715776 | bytes 10628096 | tf_op jit(solution)/shard_map/dot_general | solution.py:43
  378.5 3.0 pad_maximum_fusion
  381.6 1.8 fusion.38
  384.8 1.6 collective-permute-start.3
  389.3 18.7 %collective-permute-done.3 = bf16[640,768]{1,0:T(8,128)(2,1)S(1)} collective-permute-done((bf16[640,768]{1,0:T(8,128)(2,1)S(1)}, bf16[640,768]{1,0:T(8,128)(2,1)S(1)}, u32[]{:S(2)}, u32[]{:S(2)}) %collective-permute-start.3) | collective-permute-done | bytes 983072 | tf_op jit(solution)/shard_map/ppermute | solution.py:413
  409.6 1.2 slice_bitcast_fusion
  411.7 1.5 collective-permute-start.4
  413.1 1.4 slice_convert_fusion.1
  418.5 92.7 %reduce-scatter.8.cloned.1.call-done = bf16[96,768]{1,0:T(8,128)(2,1)} async-done(((bf16[3072,768]{1,0:T(8,128)(2,1)}), bf16[96,768]{1,0:T(8,128)(2,1)}) %reduce-scatter.8.cloned.1.call-update) | async-done | bytes 147472 | tf_op jit(solution)/shard_map/reduce_scatter | solution.py:569
  511.1 1.6 convert_element_type.152
  512.8 113.9 %reduce-scatter.10.cloned.1.call-done = bf16[24,3968]{1,0:T(8,128)(2,1)} async-done(((bf16[768,3968]{1,0:T(8,128)(2,1)}), bf16[24,3968]{1,0:T(8,128)(2,1)}) %reduce-scatter.10.cloned.1.call-update) | async-done | bytes 190480
  626.7 1.0 convert_element_type.147
  630.1 1.4 slice.287
  631.5 1.6 slice.292
  (235 shorter events, 45.8 us)
Async XLA Ops:
  7.2 11.1 %copy-start.25 = (bf16[1,128,768]{2,1,0:T(8,128)(2,1)S(1)}, bf16[1,128,768]{2,1,0:T(8,128)(2,1)}, u32[]{:S(2)}) copy-start(bf16[1,128,768]{2,1,0:T(8,128)(2,1)} %param.22) | copy-start | bytes 589828
  7.2 11.1 %copy-start.16 = (bf16[1,512,768]{2,1,0:T(8,128)(2,1)S(1)}, bf16[1,512,768]{2,1,0:T(8,128)(2,1)}, u32[]{:S(2)}) copy-start(bf16[1,512,768]{2,1,0:T(8,128)(2,1)} %param.21) | copy-start | bytes 2359300
  7.2 11.1 %copy-start.20 = (bf16[1,192,768]{2,1,0:T(8,128)(2,1)S(1)}, bf16[1,192,768]{2,1,0:T(8,128)(2,1)}, u32[]{:S(2)}) copy-start(bf16[1,192,768]{2,1,0:T(8,128)(2,1)} %param.23) | copy-start | bytes 884740
  7.2 54.2 %all-gather.4.cloned.1.call-start = ((), (), s32[]{:S(2)}) async-start(), calls=%async_computation.3 | async-start | bytes 2715648 | tf_op jit(solution)/shard_map/all_gather | solution.py:468
  15.6 6.8 %copy-start.6 = (s32[1,4]{1,0:T(1,128)S(1)}, s32[1,4]{1,0:T(1,128)}, u32[]{:S(2)}) copy-start(s32[1,4]{1,0:T(1,128)} %param.25) | copy-start | bytes 52
  15.6 8.1 %copy-start.42 = (s32[1,1408]{1,0:T(1,128)S(1)}, s32[1,1408]{1,0:T(1,128)}, u32[]{:S(2)}) copy-start(s32[1,1408]{1,0:T(1,128)} %param.24) | copy-start | bytes 16900
  15.6 8.1 %copy-start.45 = (s32[1,384]{1,0:T(1,128)S(1)}, s32[1,384]{1,0:T(1,128)}, u32[]{:S(2)}) copy-start(s32[1,384]{1,0:T(1,128)} %param.26) | copy-start | bytes 4612
  15.6 8.2 %slice-start = ((s32[1,1408]{1,0:T(1,128)}), s32[1,1024]{1,0:T(1,128)S(1)}, s32[]{:S(2)}) async-start(s32[1,1408]{1,0:T(1,128)} %param.24), calls=%async_computation.9 | async-start | bytes 8192 | tf_op jit(solution)/shard_map/slice | solution.py:502
  15.6 130.9 %all-gather.6.cloned.1.call-start = ((), (), s32[]{:S(2)}) async-start(), calls=%async_computation.4 | async-start | bytes 6266880 | tf_op jit(solution)/shard_map/all_gather | solution.py:469
  17.5 158.9 %all-gather.8.cloned.1.call-start = ((), (), s32[]{:S(2)}) async-start(), calls=%async_computation.5 | async-start | bytes 5013504 | tf_op jit(solution)/shard_map/all_gather | solution.py:472
  18.2 392.6 %reduce-scatter.6.cloned.1.call-start = ((), (), s32[]{:S(2)}) async-start(), calls=%async_computation.6 | async-start | bytes 2715648 | tf_op jit(solution)/shard_map/reduce_scatter | solution.py:627
  19.4 31.4 %collective-permute-start = (bf16[832,768]{1,0:T(8,128)(2,1)}, bf16[832,768]{1,0:T(8,128)(2,1)}, u32[]{:S(2)}, u32[]{:S(2)}) collective-permute-start(bf16[832,768]{1,0:T(8,128)(2,1)} %pad_maximum_fusion.7), channel_id=1, source_target_pairs={{0,16},{16,0},{1,17},{17,1},{2,18},{18,2},{3,19},{19,3},{4,20},{20... | collective-permute-start | bytes 3833864 | tf_op jit(solution)/shard_map/ppermute | solution.py:413
  25.1 25.7 %copy-start.26 = (bf16[1,128,768]{2,1,0:T(8,128)(2,1)S(1)}, bf16[1,128,768]{2,1,0:T(8,128)(2,1)}, u32[]{:S(2)}) copy-start(bf16[1,128,768]{2,1,0:T(8,128)(2,1)} %param.22) | copy-start | bytes 589828
  40.8 24.3 %copy-start.18 = (bf16[2432,384]{1,0:T(8,128)(2,1)}, bf16[2432,384]{1,0:T(8,128)(2,1)S(1)}, u32[]{:S(2)}) copy-start(bf16[2432,384]{1,0:T(8,128)(2,1)S(1)} %get-tuple-element.83) | copy-start | bytes 5603332
  65.1 3.9 copy-start.12
  69.0 7.9 %copy-start = (bf16[2432,384]{1,0:T(8,128)(2,1)}, bf16[2432,384]{1,0:T(8,128)(2,1)S(1)}, u32[]{:S(2)}) copy-start(bf16[2432,384]{1,0:T(8,128)(2,1)S(1)} %convolution_convert_fusion.3.rel_ref) | copy-start | bytes 5603332
  130.5 1.3 copy-start.1
  131.8 14.7 %copy-start.27 = (bf16[1,128,768]{2,1,0:T(8,128)(2,1)S(1)}, bf16[1,128,768]{2,1,0:T(8,128)(2,1)}, u32[]{:S(2)}) copy-start(bf16[1,128,768]{2,1,0:T(8,128)(2,1)} %param.22) | copy-start | bytes 589828
  131.8 17.5 %copy-start.33 = (bf16[128,384]{1,0:T(8,128)(2,1)}, bf16[128,384]{1,0:T(8,128)(2,1)S(1)}, u32[]{:S(2)}) copy-start(bf16[128,384]{1,0:T(8,128)(2,1)S(1)} %get-tuple-element.67) | copy-start | bytes 294916
  131.9 17.4 %copy-start.29 = (bf16[512,384]{1,0:T(8,128)(2,1)}, bf16[512,384]{1,0:T(8,128)(2,1)S(1)}, u32[]{:S(2)}) copy-start(bf16[512,384]{1,0:T(8,128)(2,1)S(1)} %get-tuple-element.65) | copy-start | bytes 1179652
  132.8 13.7 %collective-permute-start.1 = (bf16[640,384]{1,0:T(8,128)(2,1)}, bf16[640,384]{1,0:T(8,128)(2,1)}, u32[]{:S(2)}, u32[]{:S(2)}) collective-permute-start(bf16[640,384]{1,0:T(8,128)(2,1)} %pad_maximum_fusion.10), channel_id=1, source_target_pairs={{0,16},{16,0},{1,17},{17,1},{2,18},{18,2},{3,19},{19,3},{4,20},{20... | collective-permute-start | bytes 1474568 | tf_op jit(solution)/shard_map/ppermute | solution.py:413
  136.3 40.2 %copy-start.43 = (f32[768]{0:T(1024)}, f32[768]{0:T(1024)S(1)}, u32[]{:S(2)}) copy-start(f32[768]{0:T(1024)S(1)} %add.204) | copy-start | bytes 9220
  136.3 73.3 %copy-start.38 = (f32[768]{0:T(1024)}, f32[768]{0:T(1024)S(1)}, u32[]{:S(2)}) copy-start(f32[768]{0:T(1024)S(1)} %mul.260) | copy-start | bytes 9220
  146.5 4.0 slice-start.1
  146.5 4.0 slice-start.2
  149.3 1.3 copy-start.9
  149.3 60.3 %copy-start.34 = (f32[640]{0:T(1024)}, f32[640]{0:T(1024)S(1)}, u32[]{:S(2)}) copy-start(f32[640]{0:T(1024)S(1)} %broadcast_multiply_fusion.1) | copy-start | bytes 7684
  150.5 59.1 %copy-start.40 = (f32[640]{0:T(1024)}, f32[640]{0:T(1024)S(1)}, u32[]{:S(2)}) copy-start(f32[640]{0:T(1024)S(1)} %fusion.65) | copy-start | bytes 7684
  186.7 1.1 copy-start.11
  186.7 1.2 copy-start.19
  186.8 5.2 copy-start.46
  189.3 2.8 slice-start.5
  189.3 2.8 slice-start.6
  191.1 12.0 %slice-start.3 = ((s8[5898240]{0:T(1024)(128)(4,1)}), s8[4194304]{0:T(1024)(128)(4,1)S(1)}, s32[]{:S(2)}) async-start(s8[5898240]{0:T(1024)(128)(4,1)} %bitcast.83), calls=%async_computation.12 | async-start | bytes 8388608
  192.0 11.2 %copy-start.21 = (bf16[640,768]{1,0:T(8,128)(2,1)}, bf16[640,768]{1,0:T(8,128)(2,1)S(1)}, u32[]{:S(2)}) copy-start(bf16[640,768]{1,0:T(8,128)(2,1)S(1)} %get-tuple-element.45) | copy-start | bytes 2949124
  192.1 11.1 %copy-start.10 = (f32[640,768]{1,0:T(8,128)S(1)}, f32[640,768]{1,0:T(8,128)}, u32[]{:S(2)}) copy-start(f32[640,768]{1,0:T(8,128)} %copy-done.9) | copy-start | bytes 5898244
  192.1 11.1 %slice-start.4 = ((s8[5898240]{0:T(1024)(128)(4,1)}), s8[1703936]{0:T(1024)(128)(4,1)S(1)}, s32[]{:S(2)}) async-start(s8[5898240]{0:T(1024)(128)(4,1)} %bitcast.83), calls=%async_computation.13 | async-start | bytes 3407872
  210.4 1.3 copy-start.7
  210.4 1.3 copy-start.36
  212.5 13.7 %collective-permute-start.2 = (bf16[640,384]{1,0:T(8,128)(2,1)}, bf16[640,384]{1,0:T(8,128)(2,1)}, u32[]{:S(2)}, u32[]{:S(2)}) collective-permute-start(bf16[640,384]{1,0:T(8,128)(2,1)} %constant_dynamic-slice_fusion.6), channel_id=1, source_target_pairs={{0,16},{16,0},{1,17},{17,1},{2,18},{18,2},{3,19},{19,3},{4,20},{20... | collective-permute-start | bytes 1474568 | tf_op jit(solution)/shard_map/ppermute | solution.py:413
  316.8 1.1 copy-start.2
  317.9 1.0 copy-start.4
  319.9 5.5 copy-start.3
  325.5 3.4 copy-start.5
  328.9 3.5 copy-start.23
  328.9 3.5 copy-start.24
  328.9 3.5 copy-start.31
  328.9 3.5 copy-start.32
  333.8 1.1 copy-start.17
  333.8 1.1 copy-start.22
  336.7 174.5 %reduce-scatter.8.cloned.1.call-start = ((), (), s32[]{:S(2)}) async-start(), calls=%async_computation.7 | async-start | bytes 4866048 | tf_op jit(solution)/shard_map/reduce_scatter | solution.py:569
  347.6 279.2 %reduce-scatter.10.cloned.1.call-start = ((), (), s32[]{:S(2)}) async-start(), calls=%async_computation.8 | async-start | bytes 6285312
  369.0 2.4 copy-start.35
  369.0 2.4 copy-start.39
  369.0 2.4 copy-start.41
  369.0 2.4 copy-start.44
  371.4 7.1 %copy-start.14 = (bf16[768,768]{1,0:T(8,128)(2,1)S(1)}, bf16[768,768]{1,0:T(8,128)(2,1)}, u32[]{:S(2)}) copy-start(bf16[768,768]{1,0:T(8,128)(2,1)} %copy.60) | copy-start | bytes 3538948
  371.5 7.1 %copy-start.28 = (bf16[768,128]{1,0:T(8,128)(2,1)S(1)}, bf16[768,128]{1,0:T(8,128)(2,1)}, u32[]{:S(2)}) copy-start(bf16[768,128]{1,0:T(8,128)(2,1)} %reshape.299) | copy-start | bytes 589828
  381.5 1.9 copy-start.13
  384.1 2.3 copy-start.15
  384.8 23.2 %collective-permute-start.3 = (bf16[640,768]{1,0:T(8,128)(2,1)S(1)}, bf16[640,768]{1,0:T(8,128)(2,1)S(1)}, u32[]{:S(2)}, u32[]{:S(2)}) collective-permute-start(bf16[640,768]{1,0:T(8,128)(2,1)S(1)} %add_convert_fusion), channel_id=1, source_target_pairs={{0,16},{16,0},{1,17},{17,1},{2,18},{18,2},{3,19},{19,3},{4,20},{20... | collective-permute-start | bytes 2949128 | tf_op jit(solution)/shard_map/ppermute | solution.py:413
  388.6 19.3 %copy-start.8 = (f32[640,768]{1,0:T(8,128)S(1)}, f32[640,768]{1,0:T(8,128)}, u32[]{:S(2)}) copy-start(f32[640,768]{1,0:T(8,128)} %copy-done.7) | copy-start | bytes 5898244
  388.6 19.3 %copy-start.37 = (f32[640]{0:T(1024)S(1)}, f32[640]{0:T(1024)}, u32[]{:S(2)}) copy-start(f32[640]{0:T(1024)} %copy-done.36) | copy-start | bytes 7684
  411.7 4.9 collective-permute-start.4
  (1 other events, 0.7 us)
Sparse Core Ops, SparseCore 0:
  15.7 45.6 all-gather.3
  63.7 58.4 all-gather.5
  124.5 51.8 all-gather.7
  336.8 62.0 reduce-scatter.5
  405.1 105.9 reduce-scatter.7
  516.8 109.8 reduce-scatter.9

commit v2 on v1

--- a/solution.py
+++ b/solution.py
@@ -27,6 +27,7 @@
 SCORE_SCALE = 0.125
 EXP2_SCALE = SCORE_SCALE * 1.4426950408889634
 STEPS = NBLK + 1
+VMEM_LIMIT = 60 * 1024 * 1024
 BF = jnp.bfloat16
 F32 = jnp.float32
 
@@ -43,25 +44,15 @@
     return lax.dot_general(left, right, (((0,), (0,)), ((), ())), preferred_element_type=F32)
 
 
-def layer_norm(values, gain, shift):
-    center = values - jnp.mean(values, -1, keepdims=True)
-    spread = jnp.mean(center * center, -1, keepdims=True)
-    return center * lax.rsqrt(spread + EPSILON) * gain + shift
-
-
-def gelu_tanh(values):
-    return (
-        0.5
-        * values
-        * (1.0 + jnp.tanh(0.7978845608028654 * (values + 0.044715 * values * values * values)))
-    )
-
-
 def sinusoid(row_count, width_all, farthest):
-    distance = farthest - jnp.arange(row_count).astype(F32)
+    fine = DH
     frequency = 10000.0 ** (-jnp.arange(0, width_all, 2).astype(F32) / width_all)
-    angles = distance[:, None] * frequency[None, :]
-    return jnp.concatenate([jnp.sin(angles), jnp.cos(angles)], 1)
+    starts = (farthest - fine * jnp.arange(row_count // fine)).astype(F32)
+    far = starts[:, None, None] * frequency
+    near = jnp.arange(fine).astype(F32)[None, :, None] * frequency
+    sines = jnp.sin(far) * jnp.cos(near) - jnp.cos(far) * jnp.sin(near)
+    cosines = jnp.cos(far) * jnp.cos(near) + jnp.sin(far) * jnp.sin(near)
+    return jnp.concatenate([sines, cosines], 2).reshape(row_count, width_all)
 
 
 def split_low(values):
@@ -99,7 +90,7 @@
     lhs_ref,
     qr_ref,
 ):
-    step = pl.program_id(1)
+    step = pl.program_id(0)
 
     @pl.when(step == 0)
     def _():
@@ -204,9 +195,7 @@
     att_ref,
     inv_ref,
     exp_ref,
-    dq_ref,
-    dk_ref,
-    dv_ref,
+    dqkv_ref,
     drel_ref,
     dpar_ref,
     kcat_ref,
@@ -222,7 +211,7 @@
     accw_ref,
     accr_ref,
 ):
-    step = pl.program_id(1)
+    step = pl.program_id(0)
 
     @pl.when(step == 0)
     def _():
@@ -303,50 +292,49 @@
     same = jnp.where(first, same_sums[0], same_sums[1])
     other = jnp.where(first, other_sums[0], other_sums[1])
     grad_s = same * par_ref[3:4, :] + other * par_ref[4:5, :]
-    dq_ref[pl.ds(row, BLOCK), :] = (grad_w + grad_r + grad_s).astype(BF)
+    dqkv_ref[pl.ds(row, BLOCK), :LANES] = (grad_w + grad_r + grad_s).astype(BF)
     for at, rows in enumerate((grad_w, grad_r, grad_s, same * query_s, other * query_s)):
         dpar_ref[at : at + 1, :] += jnp.sum(rows, 0, keepdims=True)
 
     @pl.when(step == STEPS - 1)
     def _():
-        dk_ref[...] = dkt_ref[...].T.astype(BF)
-        dv_ref[...] = dvt_ref[...].T.astype(BF)
+        dqkv_ref[MROW:, :LANES] = jnp.zeros((MEM, LANES), BF)
+        dqkv_ref[:, LANES : 2 * LANES] = dkt_ref[...].T.astype(BF)
+        dqkv_ref[:, 2 * LANES :] = dvt_ref[...].T.astype(BF)
         drel_ref[...] = drelt_ref[...].T.astype(BF)
 
 
-def attention_specs(pairs):
-    def column(rows, first):
-        return pl.BlockSpec((rows, LANES), lambda pair, step, order: (0, first + pair))
-
-    shared = pl.BlockSpec((ROWS, LANES), lambda pair, step, order: (0, 0))
-    ins = [
-        column(ROWS, 0),
-        column(ROWS, pairs),
-        column(ROWS, 2 * pairs),
-        column(REL_ROWS, 0),
-        shared,
-        column(8, 0),
-    ]
-    exps = pl.BlockSpec(
-        (None, None, 2, BLOCK, KEYS), lambda pair, step, order: (pair, step, 0, 0, 0)
-    )
-    return column, ins, exps
-
-
-PARAMS = dict(
-    dimension_semantics=("arbitrary", "arbitrary"), vmem_limit_bytes=48 * 1024 * 1024
-)
-
-
-def attention_forward(order, qkv, rel, marks, par):
-    pairs = rel.shape[1] // LANES
-    column, ins, exps = attention_specs(pairs)
-    width = pairs * LANES
+def column(rows, at):
+    return pl.BlockSpec((rows, LANES), lambda step, order: (0, at))
+
+
+def attention_specs(pair, first):
+    ins = [column(ROWS, first + at) for at in range(3)]
+    ins += [column(REL_ROWS, pair), column(ROWS, 0), column(8, pair)]
+    exps = pl.BlockSpec((None, 2, BLOCK, KEYS), lambda step, order: (step, 0, 0, 0))
+    return ins, exps
+
+
+def settings(passes):
+    return dict(
+        compiler_params=pltpu.CompilerParams(
+            dimension_semantics=("arbitrary",), vmem_limit_bytes=40 * 1024 * 1024
+        ),
+        cost_estimate=pl.CostEstimate(
+            flops=passes * 4 * MROW * KEYS * BLOCK,
+            bytes_accessed=STEPS * 2 * BLOCK * KEYS * 2,
+            transcendentals=2 * MROW * KEYS,
+        ),
+    )
+
+
+def attention_forward(pair, first, order, qkv, rel, marks, par):
+    ins, exps = attention_specs(pair, first)
     return pl.pallas_call(
         forward_kernel,
         grid_spec=pltpu.PrefetchScalarGridSpec(
             num_scalar_prefetch=1,
-            grid=(pairs, STEPS),
+            grid=(STEPS,),
             in_specs=ins,
             out_specs=[column(MROW, 0), exps, column(MROW, 0)],
             scratch_shapes=[
@@ -358,28 +346,24 @@
             ],
         ),
         out_shape=[
-            jax.ShapeDtypeStruct((MROW, width), BF),
-            jax.ShapeDtypeStruct((pairs, STEPS, 2, BLOCK, KEYS), BF),
-            jax.ShapeDtypeStruct((MROW, width), F32),
+            jax.ShapeDtypeStruct((MROW, LANES), BF),
+            pltpu.HBM((STEPS, 2, BLOCK, KEYS), BF),
+            jax.ShapeDtypeStruct((MROW, LANES), F32),
         ],
-        compiler_params=pltpu.CompilerParams(**PARAMS),
+        **settings(16),
     )(order, qkv, qkv, qkv, rel, marks, par)
 
 
-def attention_backward(order, qkv, rel, marks, par, grad, att, inverse, exps_in):
-    pairs = rel.shape[1] // LANES
-    column, ins, exps = attention_specs(pairs)
-    width = pairs * LANES
+def attention_backward(pair, first, order, qkv, rel, marks, par, grad, att, inverse, exps_in):
+    ins, exps = attention_specs(pair, first)
     return pl.pallas_call(
         backward_kernel,
         grid_spec=pltpu.PrefetchScalarGridSpec(
             num_scalar_prefetch=1,
-            grid=(pairs, STEPS),
+            grid=(STEPS,),
             in_specs=ins + [column(MROW, 0)] * 3 + [exps],
             out_specs=[
-                column(MROW, 0),
-                column(ROWS, 0),
-                column(ROWS, 0),
+                pl.BlockSpec((ROWS, 3 * LANES), lambda step, order: (0, 0)),
                 column(REL_ROWS, 0),
                 column(8, 0),
             ],
@@ -399,18 +383,272 @@
             ],
         ),
         out_shape=[
-            jax.ShapeDtypeStruct((MROW, width), BF),
-            jax.ShapeDtypeStruct((ROWS, width), BF),
-            jax.ShapeDtypeStruct((ROWS, width), BF),
-            jax.ShapeDtypeStruct((REL_ROWS, width), BF),
-            jax.ShapeDtypeStruct((8, width), F32),
+            jax.ShapeDtypeStruct((ROWS, 3 * LANES), BF),
+            jax.ShapeDtypeStruct((REL_ROWS, LANES), BF),
+            jax.ShapeDtypeStruct((8, LANES), F32),
         ],
-        compiler_params=pltpu.CompilerParams(**PARAMS),
+        **settings(24),
     )(order, qkv, qkv, qkv, rel, marks, par, grad, att, inverse, exps_in)
+
+
+CHUNKS = 2
+
+
+def norm_parts(values):
+    center = values - jnp.mean(values, -1, keepdims=True)
+    spread = jnp.mean(center * center, -1, keepdims=True)
+    scale = lax.rsqrt(spread + EPSILON)
+    return center * scale, scale
+
+
+def norm_pull(grad, unit, scale, gain):
+    grad = grad * gain
+    mean = jnp.mean(grad, -1, keepdims=True)
+    slope = jnp.mean(grad * unit, -1, keepdims=True)
+    return (grad - mean - unit * slope) * scale
+
+
+def middle_kernel(
+    attn_ref,
+    hidden_ref,
+    query_ref,
+    grad_hidden_ref,
+    grad_query_ref,
+    w_out_ref,
+    w_inner_ref,
+    w_outer_ref,
+    inner_bias_ref,
+    small_ref,
+    result_ref,
+    grad_sum_ref,
+    grad_attn_ref,
+    gw_ref,
+    gb_inner_ref,
+    g_small_ref,
+    unit_ref,
+    scale_ref,
+    low_ref,
+    low_t_ref,
+    act_ref,
+    slope_ref,
+    sum_ref,
+    grad_ref,
+    grad_low_ref,
+    back_ref,
+):
+    step = pl.program_id(0)
+    rows, width = attn_ref.shape
+    tiles = act_ref.shape[1] // width
+    half = hidden_ref.shape[0]
+    cut = rows // CHUNKS
+    gain_one, shift_one = small_ref[0:1, :], small_ref[1:2, :]
+    gain_two, shift_two = small_ref[2:3, :], small_ref[3:4, :]
+    parts = [slice(at * cut, at * cut + cut) for at in range(CHUNKS)]
+
+    @pl.when(step == 0)
+    def _():
+        sum_ref[...] = product(attn_ref[...], w_out_ref[...])
+        sum_ref[:half, :] += hidden_ref[...].astype(F32)
+        sum_ref[half:, :] += query_ref[...].astype(F32)
+        for part in parts:
+            unit, scale = norm_parts(sum_ref[part, :])
+            unit_ref[part, :] = unit
+            scale_ref[part, :] = jnp.broadcast_to(scale, (cut, LANES))
+            first = unit * gain_one + shift_one
+            low_ref[part, :] = first.astype(BF)
+            sum_ref[part, :] = first + small_ref[4:5, :]
+
+    place_of = jnp.where(step < tiles, step, lax.div(step - tiles, 2))
+    columns = pl.ds(pl.multiple_of(place_of * width, width), width)
+
+    @pl.when(step < tiles)
+    def _():
+        for part in parts:
+            pre = product(low_ref[part, :], w_inner_ref[...]) + inner_bias_ref[...]
+            square = pre * pre
+            bend = jnp.tanh(0.7978845608028654 * (pre + 0.044715 * square * pre))
+            half_bend = 0.5 + 0.5 * bend
+            act = (pre * half_bend).astype(BF)
+            act_ref[part, columns] = act
+            turn = 0.7978845608028654 * (1.0 + 0.134145 * square)
+            slope_ref[part, columns] = half_bend + 0.5 * pre * (1.0 - bend * bend) * turn
+            sum_ref[part, :] += product(act, w_outer_ref[...])
+
+    @pl.when(step == tiles - 1)
+    def _():
+        g_gain = g_shift = g_outer = 0.0
+        grad_ref[:half, :] = grad_hidden_ref[...].astype(F32)
+        grad_ref[half:, :] = grad_query_ref[...].astype(F32)
+        for part in parts:
+            unit, scale = norm_parts(sum_ref[part, :])
+            result_ref[part, :] = (unit * gain_two + shift_two).astype(BF)
+            grad = grad_ref[part, :]
+            g_gain += jnp.sum(grad * unit, 0, keepdims=True)
+            g_shift += jnp.sum(grad, 0, keepdims=True)
+            grad = norm_pull(grad, unit, scale, gain_two)
+            low = grad.astype(BF)
+            grad_ref[part, :] = grad
+            grad_low_ref[part, :] = low
+            g_outer += jnp.sum(low.astype(F32), 0, keepdims=True)
+        g_small_ref[...] = jnp.zeros_like(g_small_ref)
+        g_small_ref[2:3, :] = g_gain
+        g_small_ref[3:4, :] = g_shift
+        g_small_ref[4:5, :] = g_outer
+        low_t_ref[...] = low_ref[...].T
+
+    turn_back = jnp.logical_and(step >= tiles, step < 3 * tiles)
+
+    @pl.when(jnp.logical_and(turn_back, lax.rem(step - tiles, 2) == 0))
+    def _():
+        g_inner = 0.0
+        for part in parts:
+            back = inner_rows(grad_low_ref[part, :], w_outer_ref[...])
+            low = (back * slope_ref[part, columns]).astype(BF)
+            back_ref[part, :] = low
+            g_inner += jnp.sum(low.astype(F32), 0, keepdims=True)
+            grad_ref[part, :] += inner_rows(low, w_inner_ref[...])
+        gb_inner_ref[...] = g_inner
+        gw_ref[...] = product(low_t_ref[...], back_ref[...]).astype(BF)
+
+    @pl.when(jnp.logical_and(turn_back, lax.rem(step - tiles, 2) == 1))
+    def _():
+        gw_ref[...] = inner_cols(act_ref[:, columns], grad_low_ref[...]).astype(BF)
+
+    @pl.when(step == 3 * tiles)
+    def _():
+        g_gain = g_shift = 0.0
+        for part in parts:
+            unit, scale = unit_ref[part, :], scale_ref[part, 0:1]
+            grad = grad_ref[part, :]
+            g_gain += jnp.sum(grad * unit, 0, keepdims=True)
+            g_shift += jnp.sum(grad, 0, keepdims=True)
+            grad = norm_pull(grad, unit, scale, gain_one)
+            grad_sum_ref[part, :] = grad
+            grad_low_ref[part, :] = grad.astype(BF)
+        g_small_ref[0:1, :] = g_gain
+        g_small_ref[1:2, :] = g_shift
+        gw_ref[...] = inner_cols(attn_ref[...], grad_low_ref[...]).astype(BF)
+        grad_attn_ref[...] = inner_rows(grad_low_ref[...], w_out_ref[...]).astype(BF)
+
+
+def middle(attn, hidden, query, grad_hidden, grad_query, weights, inner_bias, small):
+    rows, width = attn.shape
+    tiles = inner_bias.shape[1] // width
+
+    def whole(array):
+        return pl.BlockSpec(array.shape, lambda step: (0,) * array.ndim)
+
+    def square(at):
+        return pl.BlockSpec((width, width), lambda step: (0, at(step)))
+
+    def back(step):
+        return lax.min(lax.div(lax.max(step - tiles, 0), 2), tiles - 1)
+
+    def tile(step):
+        return lax.select(step < tiles, step, back(step))
+
+    def written(step):
+        odd = lax.rem(lax.max(step - tiles, 0), 2)
+        return lax.select(step == 3 * tiles, 0, 1 + back(step) + tiles * odd)
+
+    outs = [
+        jax.ShapeDtypeStruct((rows, width), BF),
+        jax.ShapeDtypeStruct((rows, width), F32),
+        jax.ShapeDtypeStruct((rows, width), BF),
+        jax.ShapeDtypeStruct((width, (1 + 2 * tiles) * width), BF),
+        jax.ShapeDtypeStruct((1, tiles * width), F32),
+        jax.ShapeDtypeStruct((8, width), F32),
+    ]
+    return pl.pallas_call(
+        middle_kernel,
+        grid=(1 + 3 * tiles,),
+        in_specs=[whole(t) for t in (attn, hidden, query, grad_hidden, grad_query)]
+        + [
+            square(lambda step: 0),
+            square(lambda step: 1 + tile(step)),
+            square(lambda step: 1 + tiles + tile(step)),
+            pl.BlockSpec((1, width), lambda step: (0, tile(step))),
+            whole(small),
+        ],
+        out_specs=[whole(t) for t in outs[:3]]
+        + [
+            square(written),
+            pl.BlockSpec((1, width), lambda step: (0, back(step))),
+            whole(outs[5]),
+        ],
+        out_shape=outs,
+        scratch_shapes=[
+            pltpu.VMEM((rows, width), F32),
+            pltpu.VMEM((rows, LANES), F32),
+            pltpu.VMEM((rows, width), BF),
+            pltpu.VMEM((width, rows), BF),
+            pltpu.VMEM((rows, tiles * width), BF),
+            pltpu.VMEM((rows, tiles * width), F32),
+            pltpu.VMEM((rows, width), F32),
+            pltpu.VMEM((rows, width), F32),
+            pltpu.VMEM((rows, width), BF),
+            pltpu.VMEM((rows, width), BF),
+        ],
+        compiler_params=pltpu.CompilerParams(
+            dimension_semantics=("arbitrary",), vmem_limit_bytes=VMEM_LIMIT
+        ),
+        cost_estimate=pl.CostEstimate(
+            flops=12 * rows * width * width * tiles,
+            bytes_accessed=20 * width * width * tiles,
+            transcendentals=rows * width * tiles,
+        ),
+    )(attn, hidden, query, grad_hidden, grad_query, weights, weights, weights, inner_bias, small)
 
 
 def swap(values):
     return lax.ppermute(values, "seq", [(0, 1), (1, 0)])
+
+
+def bit_orders(groups):
+    high = list(range(groups.bit_length() - 2, 0, -1))
+    return high, high[-1:] + high[:-1]
+
+
+def across(values, groups, bit):
+    return lax.ppermute(values, "fsdp", [(i, i ^ (1 << bit)) for i in range(groups)])
+
+
+def merged(values, theirs, place, held, bit):
+    axis = sum(1 for other in held if other > bit)
+    return jnp.where(
+        (place >> bit) & 1 == 0,
+        jnp.stack([values, theirs], axis),
+        jnp.stack([theirs, values], axis),
+    )
+
+
+def gather_beside(one, two, groups, chunks):
+    place = lax.axis_index("fsdp")
+    order_one, order_two = bit_orders(groups)
+    order_one, order_two = order_one + [0], order_two + [0]
+    swapped = []
+    for at, (bit_one, bit_two) in enumerate(zip(order_one, order_two)):
+        left = len(order_one) - at
+        take = chunks[: -(-len(chunks) // left)] if len(chunks) >= left else []
+        chunks = chunks[len(take) :]
+        theirs = [across(one, groups, bit_one), across(two, groups, bit_two)]
+        theirs += [swap(chunk) for chunk in take]
+        theirs = lax.optimization_barrier(theirs)
+        one = merged(one, theirs[0], place, order_one[:at], bit_one)
+        two = merged(two, theirs[1], place, order_two[:at], bit_two)
+        swapped += theirs[2:]
+    bits = len(order_one)
+    return (
+        one.reshape((-1,) + one.shape[bits + 1 :]),
+        two.reshape((-1,) + two.shape[bits + 1 :]),
+        swapped,
+    )
+
+
+def shuffle(count, lanes):
+    take = jnp.arange(count * lanes)[:, None]
+    give = jnp.arange(count * lanes)[None, :]
+    return ((take % lanes) * count + take // lanes == give).astype(BF)
 
 
 def pad_to(values, count):
@@ -442,6 +680,7 @@
 ):
     side = lax.axis_index("seq")
     groups = lax.axis_size("fsdp")
+    place_at = lax.axis_index("fsdp")
     half, width = hidden.shape[1:]
     target_half = query_in.shape[1]
     memory_half = memory.shape[1]
@@ -450,30 +689,59 @@
     ffn_width = w_inner.shape[1]
     own_rows = half + target_half
 
-    def own_columns(weight):
-        return lax.dynamic_slice_in_dim(weight, side * head_width, head_width, 1)
-
-    smalls = (rel_biases, seg_embed, b_inner, b_outer, norm_gains, norm_biases)
-    small_flat = pad_to(jnp.concatenate([s.reshape(-1) for s in smalls]), shard_rows * LANES)
-    packed = jnp.concatenate(
+    def by_side(own, other, axis):
+        return jnp.where(
+            side == 0,
+            jnp.concatenate([own, other], axis),
+            jnp.concatenate([other, own], axis),
+        )
+
+    pairs = head_width // LANES
+    pair_width = 3 * LANES
+
+    def head_columns(weight, pair):
+        return lax.dynamic_slice_in_dim(weight, side * head_width + pair * LANES, LANES, 1)
+
+    def pair_columns(pair):
+        return [head_columns(weight, pair) for weight in (w_query, w_key, w_value)]
+
+    few = jnp.concatenate([rel_biases, seg_embed], 0)
+    few = jnp.pad(few, ((0, shard_rows - 5), (0, LANES - few.shape[1])))
+    quarter = half // 2
+    weights_one, weights_two, swapped = gather_beside(
+        jnp.concatenate(sum([pair_columns(pair) for pair in range(pairs - 1)], []), 1),
+        jnp.concatenate(pair_columns(pairs - 1) + [w_rel, few], 1),
+        groups,
+        [hidden[0, :quarter], hidden[0, quarter:], memory[0], query_in[0]],
+    )
+    rel_weight = weights_two[:, pair_width : pair_width + head_width]
+    few_all = weights_two[:, pair_width + head_width :].reshape(groups, shard_rows, LANES)
+    few_all = few_all[:, :5, : head_width // groups].astype(F32)
+    few_all = few_all.transpose(1, 0, 2).reshape(5, head_width)
+
+    blocks = ffn_width // width
+    spots = shuffle(blocks, LANES)
+    smalls = (b_inner, b_outer, norm_gains, norm_biases)
+    small_flat = pad_to(jnp.concatenate([t.reshape(-1) for t in smalls]), shard_rows * LANES)
+    inner_moved = lax.dot_general(
+        w_inner.reshape(shard_rows, -1, blocks * LANES),
+        spots,
+        (((2,), (1,)), ((), ())),
+        preferred_element_type=F32,
+    ).astype(BF)
+    inner_moved = inner_moved.reshape(shard_rows, -1, blocks, LANES).transpose(0, 2, 1, 3)
+    mixed = jnp.concatenate(
         [
-            own_columns(w_query),
-            own_columns(w_key),
-            own_columns(w_value),
-            w_rel,
+            w_out,
+            inner_moved.reshape(shard_rows, ffn_width),
+            w_outer.reshape(shard_rows, ffn_width),
             small_flat.reshape(shard_rows, LANES),
         ],
         1,
     )
-    packed = lax.all_gather(packed, "fsdp", axis=0, tiled=True)
-    mixed = lax.all_gather(
-        jnp.concatenate([w_out, w_inner], 1), "fsdp", axis=0, tiled=True
-    )
-    full_outer = lax.all_gather(w_outer, "fsdp", axis=0, tiled=True)
-    full_out, full_inner = mixed[:, :width], mixed[:, width:]
-    head_weights = packed[:, : 3 * head_width]
-    rel_weight = packed[:, 3 * head_width : 4 * head_width]
-    small_all = packed[:, 4 * head_width :].reshape(groups, shard_rows * LANES).astype(F32)
+    mixed, weights_one, swapped = lax.optimization_barrier((mixed, weights_one, swapped))
+    mixed = lax.all_gather(mixed, "fsdp", axis=0, tiled=True)
+    small_all = mixed[:, width + 2 * ffn_width :].reshape(groups, shard_rows * LANES).astype(F32)
 
     def unpack():
         found, at = [], 0
@@ -483,19 +751,24 @@
             at += small.size
         return found
 
-    all_biases, all_seg, inner_bias, outer_bias, gains, shifts = unpack()
-
-    mine = jnp.concatenate([hidden[0], query_in[0], memory[0]], 0)
-    theirs = swap(mine)
-    low = jnp.where(side == 0, mine, theirs)
-    high = jnp.where(side == 0, theirs, mine)
-    cuts = ((0, half), (half, own_rows), (own_rows, own_rows + memory_half))
-    stacked = jnp.concatenate([part[a:b] for a, b in cuts for part in (low, high)], 0)
-
-    qkv = product(stacked, head_weights).astype(BF)
+    inner_bias, outer_bias, gains, shifts = unpack()
+
+    cuts = ((0, half), (half, own_rows))
+    far_hidden = jnp.concatenate(swapped[:2], 0)
+    stacked = jnp.concatenate(
+        [
+            by_side(hidden[0], far_hidden, 0),
+            by_side(query_in[0], swapped[3], 0),
+            by_side(memory[0], swapped[2], 0),
+        ],
+        0,
+    )
+
+    qkv_one = product(stacked, weights_one).astype(BF)
+    qkv_two = product(stacked, weights_two[:, :pair_width]).astype(BF)
     pos_table = sinusoid(REL_ROWS, width, MEM + L - 1).astype(BF)
     rel = product(pos_table, rel_weight).astype(BF)
-    par = jnp.concatenate([all_biases, all_seg, jnp.zeros((3, head_width), F32)], 0)
+    par = jnp.concatenate([few_all, jnp.zeros((3, head_width), F32)], 0)
     order = block_order[0]
     segs = segment_ids[0]
     target_seg = lax.dynamic_slice_in_dim(segs, MEM + order[NBLK - 1] * BLOCK, BLOCK)
@@ -505,8 +778,6 @@
     marks = jnp.where(lane < 6, seg_rows[:, None] == lane % 3, (lane == 6) | (lane == 7))
     marks = jnp.where(lane == 8, invalid[:, None] == 1, marks).astype(BF)
 
-    att, exps, inverse = attention_forward(order, qkv, rel, marks, par)
-
     def rows_of(values, which):
         return jnp.concatenate(
             [
@@ -516,131 +787,137 @@
             0,
         )
 
-    def by_side(own, other, axis):
-        return jnp.where(
-            side == 0,
-            jnp.concatenate([own, other], axis),
-            jnp.concatenate([other, own], axis),
-        )
-
-    attn_rows = by_side(rows_of(att, side), swap(rows_of(att, 1 - side)), 1)
-    first_sum = product(attn_rows, full_out) + mine[:own_rows].astype(F32)
-    first_norm = layer_norm(first_sum, gains[0], shifts[0])
-    first_low = first_norm.astype(BF)
-    hidden_pre = product(first_low, full_inner) + inner_bias
-    activation = gelu_tanh(hidden_pre).astype(BF)
-    second_sum = product(activation, full_outer) + outer_bias + first_norm
-    result = layer_norm(second_sum, gains[1], shifts[1]).astype(BF)
-    grad_rows = jnp.concatenate([grad_hidden_out[0], grad_query_out[0]], 0).astype(F32)
-    second_pull = jax.vjp(layer_norm, second_sum, gains[1], shifts[1])[1]
-    grad_second, grad_gain_two, grad_shift_two = second_pull(grad_rows)
-    grad_outer_low = grad_second.astype(BF)
-    grad_b_outer = jnp.sum(grad_outer_low.astype(F32), 0)
-    grad_w_outer = inner_cols(activation, grad_outer_low)
-    gelu_pull = jax.vjp(gelu_tanh, hidden_pre)[1]
-    grad_pre = gelu_pull(inner_rows(grad_outer_low, full_outer))[0].astype(BF)
-    grad_b_inner = jnp.sum(grad_pre.astype(F32), 0)
-    grad_w_inner = inner_cols(first_low, grad_pre)
-    grad_first = grad_second + inner_rows(grad_pre, full_inner)
-    first_pull = jax.vjp(layer_norm, first_sum, gains[0], shifts[0])[1]
-    grad_sum_one, grad_gain_one, grad_shift_one = first_pull(grad_first)
-    grad_mixed = grad_sum_one.astype(BF)
-    grad_w_out = inner_cols(attn_rows, grad_mixed)
-    grad_attn = inner_rows(grad_mixed, full_out).astype(BF)
+    def pair_args(pair):
+        last = pair == pairs - 1
+        at = (0, qkv_two) if last else (3 * pair, qkv_one)
+        return (pair, at[0], order, at[1], rel, marks, par)
+
+    kept = []
+    own_att, far_att = [], []
+    for pair in range(pairs):
+        att, exps, inverse = attention_forward(*pair_args(pair))
+        kept.append((att, inverse, exps))
+        own_att.append(rows_of(att, side))
+        far_att.append(swap(rows_of(att, 1 - side)))
+    attn_rows = by_side(jnp.concatenate(own_att, 1), jnp.concatenate(far_att, 1), 1)
+    small = jnp.stack([gains[0], shifts[0], gains[1], shifts[1], outer_bias] + [outer_bias] * 3)
+    result, grad_sum_one, grad_attn, grad_weights, grad_b_inner, grad_small = middle(
+        attn_rows,
+        hidden[0],
+        query_in[0],
+        grad_hidden_out[0],
+        grad_query_out[0],
+        mixed,
+        inner_bias.reshape(width, blocks).T.reshape(1, ffn_width),
+        small,
+    )
 
     devices = 2 * groups
     out_rows = width // devices
-    token_smalls = (
-        grad_b_inner.reshape(devices, -1),
-        grad_b_outer.reshape(devices, -1),
-        jnp.stack([grad_gain_one, grad_gain_two]).reshape(2, devices, -1),
-        jnp.stack([grad_shift_one, grad_shift_two]).reshape(2, devices, -1),
-    )
+    token_sums = lax.psum_scatter(
+        grad_weights, ("seq", "fsdp"), scatter_dimension=0, tiled=True
+    )
+    out_out = token_sums[:, :width].astype(F32)
+    out_outer = token_sums[:, width + ffn_width :].reshape(blocks * out_rows, width).astype(F32)
+    inner_sums = token_sums[:, width : width + ffn_width].reshape(out_rows, blocks, -1, LANES)
+    out_inner = product(
+        inner_sums.transpose(0, 2, 1, 3).reshape(out_rows, -1, blocks * LANES), spots
+    ).reshape(out_rows, ffn_width)
+    grad_b_inner = grad_b_inner.reshape(blocks, width).T.reshape(devices, -1)
+    row_count = width // devices
     token_flat = jnp.concatenate(
-        [s if s.ndim == 2 else s.transpose(1, 0, 2).reshape(devices, -1) for s in token_smalls], 1
-    )
-    token_count = token_flat.shape[1]
-    token_flat = jnp.pad(token_flat, ((0, 0), (0, out_rows * LANES - token_count)))
-    token_packed = jnp.concatenate(
-        [grad_w_out, grad_w_inner, token_flat.reshape(width, LANES)], 1
-    ).astype(BF)
-    everywhere = ("seq", "fsdp")
-    token_sums = lax.psum_scatter(token_packed, everywhere, scatter_dimension=0, tiled=True)
-    out_outer = lax.psum_scatter(
-        grad_w_outer.astype(BF), everywhere, scatter_dimension=0, tiled=True
+        [
+            grad_b_inner.reshape(devices, -1),
+            grad_small[:5].reshape(5, devices, -1).transpose(1, 0, 2).reshape(devices, -1),
+        ],
+        1,
+    )
+    inner_count = ffn_width // devices
+
+    weights_two = weights_two[:, :pair_width]
+    weights_one, weights_two, attn_rows = lax.optimization_barrier(
+        (weights_one, weights_two, attn_rows)
+    )
+    far_one, far_two = swap(weights_one), swap(weights_two)
+
+    def pair_grad(pair, which):
+        at = which * head_width + pair * LANES
+        return lax.dynamic_slice_in_dim(grad_attn, at, LANES, 1)
+
+    far_grads = [swap(pair_grad(pair, 1 - side)) for pair in range(pairs)]
+
+    def sum_message(message):
+        message = lax.all_to_all(message, "fsdp", split_axis=0, concat_axis=0, tiled=True)
+        return jnp.sum(message.astype(F32), 0)
+
+    own_rows_grads, far_rows_grads, sums, few_grads = [], [], [], []
+    for pair in range(pairs):
+        own, far = pair_grad(pair, side), far_grads[pair]
+        if pair:
+            own, message, sums = lax.optimization_barrier((own, message, sums))
+            sums.append(sum_message(message))
+        head_grad = jnp.concatenate([by_side(own[a:b], far[a:b], 0) for a, b in cuts], 0)
+        dqkv, drel, dpar = attention_backward(*pair_args(pair), head_grad, *kept[pair])
+        if pair == pairs - 1:
+            dqkv, sums = lax.optimization_barrier((dqkv, sums))
+        few_grads.append(dpar[:5])
+        own_rows_grads.append(rows_of(dqkv, side))
+        far_rows_grads.append(swap(rows_of(dqkv, 1 - side)))
+        grad_pair = inner_cols(stacked, dqkv).astype(BF)
+        grad_pair = grad_pair.reshape(2, groups, out_rows, pair_width).transpose(1, 0, 2, 3)
+        message = jnp.concatenate(
+            [
+                grad_pair.reshape(groups, shard_rows, pair_width),
+                inner_cols(pos_table, drel).astype(BF).reshape(groups, shard_rows, LANES),
+            ],
+            2,
+        )
+        if pair == 0:
+            token_flat = token_flat.reshape(2, groups, -1).transpose(1, 0, 2).astype(BF)
+            extra = ((0, 0), (0, 6), (0, pair_width + LANES - token_flat.shape[2]))
+            message = jnp.concatenate([message, jnp.pad(token_flat, extra)], 1)
+        if pair == pairs - 1:
+            few = jnp.concatenate(few_grads, 1).reshape(5, groups, head_width // groups)
+            few = few.transpose(1, 0, 2).reshape(groups, 1, -1).astype(BF)
+            few = jnp.pad(few, ((0, 0), (0, 7), (0, pair_width + LANES - few.shape[2])))
+            message = jnp.concatenate([message, few], 1)
+    sums.append(sum_message(message))
+
+    early = slice(0, pairs - 1)
+    grad_own = grad_sum_one + inner_rows(
+        jnp.concatenate(own_rows_grads + far_rows_grads[early], 1),
+        jnp.concatenate([weights_one, weights_two, far_one], 1),
+    )
+    grad_own = grad_own + inner_rows(far_rows_grads[-1], far_two)
+
+    both_sums = jnp.concatenate([t[:shard_rows, :pair_width] for t in sums], 1)
+    own_sum = lax.dynamic_slice_in_dim(both_sums, side * out_rows, out_rows, 0)
+    far_sum = lax.dynamic_slice_in_dim(both_sums, (1 - side) * out_rows, out_rows, 0)
+    far_sum = swap(far_sum.astype(BF)).astype(F32)
+    small_sums = lax.dynamic_index_in_dim(sums[0], shard_rows + side, 0, False)
+    small_sums += swap(
+        lax.dynamic_index_in_dim(sums[0], shard_rows + 1 - side, 0, False).astype(BF)
     ).astype(F32)
-    token_sums = token_sums.astype(F32)
-    out_out = token_sums[:, :width]
-    out_inner = token_sums[:, width : width + ffn_width]
-    small_sums = token_sums[:, width + ffn_width :].reshape(-1)
-    inner_count, row_count = ffn_width // devices, width // devices
     out_b_inner = small_sums[:inner_count]
-    at = inner_count
-    out_b_outer = small_sums[at : at + row_count]
-    at += row_count
-    out_gains = small_sums[at : at + 2 * row_count].reshape(2, row_count)
-    at += 2 * row_count
-    out_shifts = small_sums[at : at + 2 * row_count].reshape(2, row_count)
-
-    own_grad = lax.dynamic_slice_in_dim(grad_attn, side * head_width, head_width, 1)
-    far_grad = swap(lax.dynamic_slice_in_dim(grad_attn, (1 - side) * head_width, head_width, 1))
-    head_grad = jnp.concatenate(
-        [by_side(own_grad[a:b], far_grad[a:b], 0) for a, b in cuts[:2]], 0
-    )
-    dq, dk, dv, drel, dpar = attention_backward(
-        order, qkv, rel, marks, par, head_grad, att, inverse, exps
-    )
-
-    weight_q = head_weights[:, :head_width]
-    weight_k = head_weights[:, head_width : 2 * head_width]
-    weight_v = head_weights[:, 2 * head_width :]
-
-    def back_rows(which):
-        return (
-            inner_rows(rows_of(dq, which), weight_q)
-            + jnp.pad(
-                inner_rows(
-                    lax.dynamic_slice_in_dim(dk, which * half, half, 0), weight_k
-                )
-                + inner_rows(
-                    lax.dynamic_slice_in_dim(dv, which * half, half, 0), weight_v
-                ),
-                ((0, target_half), (0, 0)),
-            )
-        )
-
-    far_rows = swap(back_rows(1 - side).astype(BF)).astype(F32)
-    grad_own = grad_sum_one + back_rows(side) + far_rows
-
-    grad_head = jnp.concatenate(
-        [inner_cols(stacked[:MROW], dq), inner_cols(stacked, dk), inner_cols(stacked, dv)], 1
-    ).astype(BF)
-    grad_head = grad_head.reshape(2, groups, out_rows, 3 * head_width)
-    grad_head = grad_head.transpose(1, 0, 2, 3).reshape(width, 3 * head_width)
-    grad_rel = inner_cols(pos_table, drel).astype(BF)
-    bias_count = head_width // groups
-    head_flat = dpar[:5].reshape(5, groups, bias_count).transpose(1, 0, 2).reshape(groups, -1)
-    head_flat = jnp.pad(head_flat, ((0, 0), (0, shard_rows * LANES - 5 * bias_count)))
-    head_packed = jnp.concatenate(
-        [grad_head, grad_rel, head_flat.reshape(width, LANES).astype(BF)], 1
-    )
-    head_sums = lax.psum_scatter(head_packed, "fsdp", scatter_dimension=0, tiled=True)
-    own_sum = lax.dynamic_slice_in_dim(head_sums, side * out_rows, out_rows, 0)
-    far_sum = lax.dynamic_slice_in_dim(head_sums, (1 - side) * out_rows, out_rows, 0)
-    own_sum = own_sum[:, : 3 * head_width].astype(F32)
-    far_sum = swap(far_sum[:, : 3 * head_width]).astype(F32)
+    out_rest = small_sums[inner_count : inner_count + 5 * row_count].reshape(5, row_count)
+    out_gains, out_shifts, out_b_outer = out_rest[0:4:2], out_rest[1:4:2], out_rest[4]
+
+    def weight_rows(values, which):
+        return [
+            values[:, pair * pair_width + which * LANES :][:, :LANES] for pair in range(pairs)
+        ]
+
     out_query, out_key, out_value = (
         by_side(
-            own_sum[:, at * head_width : (at + 1) * head_width],
-            far_sum[:, at * head_width : (at + 1) * head_width],
+            jnp.concatenate(weight_rows(own_sum, which), 1),
+            jnp.concatenate(weight_rows(far_sum, which), 1),
             1,
         )
-        for at in range(3)
-    )
-    out_rel = head_sums[:, 3 * head_width : 4 * head_width].astype(F32)
-    small_head = head_sums[:, 4 * head_width :].reshape(-1).astype(F32)
-    out_biases = small_head[: 3 * bias_count].reshape(3, bias_count)
-    out_seg = small_head[3 * bias_count : 5 * bias_count].reshape(2, bias_count)
+        for which in range(3)
+    )
+    out_rel = jnp.concatenate([t[:shard_rows, pair_width:] for t in sums], 1)
+    few_sum = sums[-1][shard_rows, : 5 * (head_width // groups)].reshape(5, -1)
+    out_biases, out_seg = few_sum[:3], few_sum[3:]
     return (
         result[None, :half],
         result[None, half:],

time: 651 us -> 409 us (0.63)
  waiting for transfers between devices: 281 us -> 36.4 us
  matrix products: 89.3 us -> 30.4 us
  Pallas kernels: 142 us -> 184 us
  starting transfers between devices: 9.46 us -> 45.6 us
  other arithmetic: 47.1 us -> 36 us
    unnamed x7 -> x2, waiting for transfers between devices: 115 us -> 0.03 us
    reduce_scatter x2 -> x1, waiting for transfers between devices: 92.7 us -> 0.01 us  [shards(): lax.psum_scatter(grad_weights, ('seq', 'fsdp'), scatter_dimension=0, tile...]
    pallas_call x0 -> x1, Pallas kernels: none -> 41 us  [middle(): pl.pallas_call(middle_kernel, grid=(1 + 3 * tiles,), in_specs=[whole(t) f...]
    ppermute x5 -> x17, waiting for transfers between devices: 50.8 us -> 26.7 us  [swap(): return lax.ppermute(values, 'seq', [(0, 1), (1, 0)])]
    all_gather x3 -> x1, waiting for transfers between devices: 23 us -> 0.01 us  [shards(): mixed = lax.all_gather(mixed, 'fsdp', axis=0, tiled=True)]
    dot_general x7 -> x6, matrix products: 34.8 us -> 11.9 us  [inner_cols(): lax.dot_general(left, right, (((0,), (0,)), ((), ())), preferred_element_...]
    dot_general x5 -> x4, matrix products: 30.9 us -> 8.17 us  [product(): return jnp.dot(left, right, preferred_element_type=F32)]
    all_to_all x0 -> x3, starting transfers between devices: none -> 17.1 us  [sum_message(): lax.all_to_all(message, 'fsdp', split_axis=0, concat_axis=0, tiled=True)]
  transfers between devices with their start and end apart: 11 -> 30, of which waited for: 8 -> 10; matrix products, arithmetic and copies ran while one was open for 18% -> 23% of each run, Pallas kernels for 8% -> 46%
where the time goes in v2:
time: 409 us; the launch traced here: 402 us
  Pallas kernels  184 us (45%)
  local copies, waits for them, and re-layouts  52.8 us (13%)
  starting transfers between devices  45.6 us (11%)
  waiting for transfers between devices  36.4 us (9%)
  other arithmetic  36 us (9%)
  matrix products  30.4 us (7%)
  between operations  16.5 us (4%)
    pallas_call x3, Pallas kernels, attention_backward(): pl.pallas_call(backward_kernel, grid_spec=pltpu.PrefetchScalarGridSpec(nu...  87.5 us
    pallas_call x3, Pallas kernels, attention_forward(): pl.pallas_call(forward_kernel, grid_spec=pltpu.PrefetchScalarGridSpec(num...  55.7 us
    pallas_call x1, Pallas kernels, middle(): pl.pallas_call(middle_kernel, grid=(1 + 3 * tiles,), in_specs=[whole(t) f...  41 us
    ppermute x17, waiting for transfers between devices, swap(): return lax.ppermute(values, 'seq', [(0, 1), (1, 0)])  26.7 us
    unnamed x132, local copies, waits for them, and re-layouts  23.5 us
    ppermute x17, starting transfers between devices, swap(): return lax.ppermute(values, 'seq', [(0, 1), (1, 0)])  18 us
    all_to_all x3, starting transfers between devices, sum_message(): lax.all_to_all(message, 'fsdp', split_axis=0, concat_axis=0, tiled=True)  17.1 us
    dot_general x6, matrix products, inner_cols(): lax.dot_general(left, right, (((0,), (0,)), ((), ())), preferred_element_...  11.9 us
  transfers between devices with their start and end apart: 30, of which 10 were waited for; matrix products, arithmetic and copies ran while one was open for 23% of the time, Pallas kernels for 46%

profile of v2, /device:TPU:0, one launch (start us, length us, event | category | flops | bytes accessed | tf_op | source)
XLA Modules:
  0.0 402.0 jit_solution(1267808735572279380)
XLA Ops:
  11.6 4.0 %collective-permute-start = (bf16[48,768]{1,0:T(8,128)(2,1)S(1)}, bf16[48,768]{1,0:T(8,128)(2,1)S(1)}, u32[]{:S(2)}, u32[]{:S(2)}) collective-permute-start(bf16[48,768]{1,0:T(8,128)(2,1)S(1)} %constant_dynamic-update-slice_fusion), channel_id=1, source_target_pairs={{0,8},{1,9},{2,10},{3,11},{4,12},{5,13},{6,14},{7,15},{8,0},{9,1},... | collective-permute-start | bytes 221192 | tf_op jit(solution)/shard_map/ppermute | solution.py:613
  17.1 1.6 collective-permute-start.1
  18.7 1.2 slice_bitcast_fusion.3
  19.9 1.6 collective-permute-start.2
  22.0 1.5 collective-permute-start.8
  23.5 1.5 fusion.8
  26.8 5.2 %collective-permute-done.2 = bf16[256,768]{1,0:T(8,128)(2,1)S(1)} collective-permute-done((bf16[256,768]{1,0:T(8,128)(2,1)S(1)}, bf16[256,768]{1,0:T(8,128)(2,1)S(1)}, u32[]{:S(2)}, u32[]{:S(2)}) %collective-permute-start.2) | collective-permute-done | bytes 393248 | tf_op jit(solution)/shard_map/ppermute | solution.py:604
  32.5 1.6 collective-permute-start.3
  34.2 6.3 %collective-permute-done.5 = bf16[256,768]{1,0:T(8,128)(2,1)} collective-permute-done((bf16[256,768]{1,0:T(8,128)(2,1)S(1)}, bf16[256,768]{1,0:T(8,128)(2,1)}, u32[]{:S(2)}, u32[]{:S(2)}) %collective-permute-start.5) | collective-permute-done | bytes 393248 | tf_op jit(solution)/shard_map/ppermute | solution.py:604
  40.6 1.6 collective-permute-start.7
  43.1 3.7 collective-permute-done.8
  46.9 2.2 collective-permute-done.6
  52.7 2.7 maximum_select_fusion.2
  57.7 3.0 subtract_convert_fusion
  60.7 1.7 select_convert_fusion.kx_ref
  64.0 1.5 maximum_select_fusion.6
  65.5 1.5 maximum_select_fusion.5
  67.1 2.0 maximum_select_fusion
  69.1 2.1 convolution_convert_fusion.rel_ref
  71.2 4.1 %convolution_convert_fusion.1.q_ref.k_ref.v_ref = bf16[1664,768]{1,0:T(8,128)(2,1)S(1)} fusion(bf16[768,768]{1,0:T(8,128)(2,1)} %bitcast.31, bf16[384,768]{1,0:T(8,128)(2,1)S(1)} %maximum_select_fusion.5, bf16[256,768]{1,0:T(8,128)(2,1)S(1)} %maximum_select_fusion.6, bf16[1024,768]{1,0:T(8,128)(2,1)S(1)} %maximum_select_fusion), kind=kOutput, calls=%fused_computation.4 | convolution fusion | flops 1971879936 | bytes 6291456 | tf_op jit(solution)/shard_map/dot_general | solution.py:36
  75.4 18.5 %shard_map.332 = (bf16[1280,128]{1,0:T(8,128)(2,1)S(1)}, bf16[5,2,256,1408]{3,2,1,0:T(8,128)(2,1)}, f32[1280,128]{1,0:T(8,128)S(1)}) custom-call(s32[4]{0:T(128)S(1)} %bitcast.128, bf16[1664,768]{1,0:T(8,128)(2,1)S(1)} %convolution_convert_fusion.1.q_ref.k_ref.v_ref, bf16[1664,768]{1,0:T(8,128)(2,1)S(1)} %convolution_convert_fusion.1.q_ref.k_ref.v_ref, ...), custom_call_target="tpu_custom_call" | custom-call | flops 29527900160 | bytes 7208960 | tf_op jit(solution)/shard_map/pallas_call | solution.py:333
  94.7 1.5 collective-permute-start.12
  96.2 18.7 %shard_map.333 = (bf16[1280,128]{1,0:T(8,128)(2,1)S(1)}, bf16[5,2,256,1408]{3,2,1,0:T(8,128)(2,1)}, f32[1280,128]{1,0:T(8,128)S(1)}) custom-call(s32[4]{0:T(128)S(1)} %bitcast.129, bf16[1664,768]{1,0:T(8,128)(2,1)S(1)} %convolution_convert_fusion.1.q_ref.k_ref.v_ref, bf16[1664,768]{1,0:T(8,128)(2,1)S(1)} %convolution_convert_fusion.1.q_ref.k_ref.v_ref, ...), custom_call_target="tpu_custom_call" | custom-call | flops 29527900160 | bytes 7208960 | tf_op jit(solution)/shard_map/pallas_call | solution.py:333
  115.0 1.5 convolution_convert_fusion.2.q_ref.k_ref.v_ref
  116.5 18.6 %shard_map.334 = (bf16[1280,128]{1,0:T(8,128)(2,1)S(1)}, bf16[5,2,256,1408]{3,2,1,0:T(8,128)(2,1)}, f32[1280,128]{1,0:T(8,128)S(1)}) custom-call(s32[4]{0:T(128)S(1)} %bitcast.130, bf16[1664,384]{1,0:T(8,128)(2,1)S(1)} %convolution_convert_fusion.2.q_ref.k_ref.v_ref, bf16[1664,384]{1,0:T(8,128)(2,1)S(1)} %convolution_convert_fusion.2.q_ref.k_ref.v_ref, ...), custom_call_target="tpu_custom_call" | custom-call | flops 29527900160 | bytes 7208960 | tf_op jit(solution)/shard_map/pallas_call | solution.py:333
  136.7 1.5 collective-permute-start.14
  138.1 4.1 %collective-permute-done.13 = bf16[640,128]{1,0:T(8,128)(2,1)S(1)} collective-permute-done((bf16[640,128]{1,0:T(8,128)(2,1)S(1)}, bf16[640,128]{1,0:T(8,128)(2,1)S(1)}, u32[]{:S(2)}, u32[]{:S(2)}) %collective-permute-start.13) | collective-permute-done | bytes 163872 | tf_op jit(solution)/shard_map/ppermute | solution.py:604
  142.3 2.7 collective-permute-done.14
  146.9 1.5 collective-permute-start.22
  151.9 41.0 %shard_map.335 = (bf16[640,768]{1,0:T(8,128)(2,1)}, f32[640,768]{1,0:T(8,128)}, bf16[640,768]{1,0:T(8,128)(2,1)}, bf16[768,6912]{1,0:T(8,128)(2,1)}, f32[1,3072]{1,0:T(1,128)}, /*index=5*/f32[8,768]{1,0:T(8,128)}) custom-call(bf16[640,768]{1,0:T(8,128)(2,1)} %broadcast_select_fusion.attn_ref, bf16[512,768]{1,0:T(8,128)(2,1)} %bitcast.138, ...), custom_call_target="tpu_custom_call" | custom-call | flops 18119393280 | bytes 47185920 | tf_op jit(solution)/shard_map/pallas_call | solution.py:562
  192.9 2.1 slice_bitcast_fusion.1
  195.1 1.6 slice_bitcast_fusion.5
  198.8 1.6 collective-permute-start.16
  201.1 4.0 collective-permute-done.15
  206.9 1.9 copy-done.8
  209.9 29.8 %shard_map.336 = (bf16[1664,384]{1,0:T(8,128)(2,1)S(1)}, bf16[2432,128]{1,0:T(8,128)(2,1)S(1)}, f32[8,128]{1,0:T(8,128)S(1)}) custom-call(s32[4]{0:T(128)S(1)} %bitcast.131, bf16[1664,768]{1,0:T(8,128)(2,1)S(1)} %copy-done.8, bf16[1664,768]{1,0:T(8,128)(2,1)S(1)} %copy-done.8, bf16[1664,768]{1,0:T(8,128)(2,1)S(1)} %copy-done.8, ...), custom_call_target="tpu_custom_call" | custom-call | flops 44291850240 | bytes 7208960 | tf_op jit(solution)/shard_map/pallas_call | solution.py:359
  239.8 1.6 convolution_convert_fusion.5
  242.0 1.2 convolution_convert_fusion.9
  245.6 4.7 %all-to-all-start = ((bf16[16,56,512]{2,1,0:T(8,128)(2,1)}), bf16[16,56,512]{2,1,0:T(8,128)(2,1)}, u32[]{:S(2)}, u32[]{:S(2)}) async-start(bf16[16,56,512]{2,1,0:T(8,128)(2,1)} %fusion.12), calls=%async_computation | async-start | bytes 1835008 | tf_op jit(solution)/shard_map/all_to_all | solution.py:850
  254.0 1.5 copy-done.5
  255.5 1.7 copy-done.9
  257.3 29.4 %shard_map.337 = (bf16[1664,384]{1,0:T(8,128)(2,1)S(1)}, bf16[2432,128]{1,0:T(8,128)(2,1)S(1)}, f32[8,128]{1,0:T(8,128)S(1)}) custom-call(s32[4]{0:T(128)S(1)} %bitcast.132, bf16[1664,768]{1,0:T(8,128)(2,1)S(1)} %copy-done.9, bf16[1664,768]{1,0:T(8,128)(2,1)S(1)} %copy-done.9, bf16[1664,768]{1,0:T(8,128)(2,1)S(1)} %copy-done.9, ...), custom_call_target="tpu_custom_call" | custom-call | flops 44291850240 | bytes 7208960 | tf_op jit(solution)/shard_map/pallas_call | solution.py:359
  286.9 1.1 copy-done.25
  288.3 1.6 convolution_convert_fusion.4
  295.6 1.2 convolution_convert_fusion.8
  298.0 2.1 convert_reduce_fusion.1
  300.1 6.3 %all-to-all-start.1 = ((bf16[16,48,512]{2,1,0:T(8,128)(2,1)}), bf16[16,48,512]{2,1,0:T(8,128)(2,1)}, u32[]{:S(2)}, u32[]{:S(2)}) async-start(bf16[16,48,512]{2,1,0:T(8,128)(2,1)} %pad_maximum_fusion.2), calls=%async_computation.1 | async-start | bytes 1572864 | tf_op jit(solution)/shard_map/all_to_all | solution.py:850
  306.6 1.3 copy-done.2
  307.9 1.5 copy-done.6
  309.4 3.0 copy-done.10
  312.4 28.3 %shard_map.338 = (bf16[1664,384]{1,0:T(8,128)(2,1)S(1)}, bf16[2432,128]{1,0:T(8,128)(2,1)S(1)}, f32[8,128]{1,0:T(8,128)S(1)}) custom-call(s32[4]{0:T(128)S(1)} %bitcast.133, bf16[1664,384]{1,0:T(8,128)(2,1)S(1)} %copy-done.2, bf16[1664,384]{1,0:T(8,128)(2,1)S(1)} %copy-done.2, bf16[1664,384]{1,0:T(8,128)(2,1)S(1)} %copy-done.2, ...), custom_call_target="tpu_custom_call" | custom-call | flops 44291850240 | bytes 7208960 | tf_op jit(solution)/shard_map/pallas_call | solution.py:359
  341.0 3.4 convolution_convert_fusion.7
  344.4 1.9 convert_reduce_fusion.2
  347.8 3.0 convolution_convert_fusion.3
  352.1 6.1 %all-to-all-start.2 = ((bf16[16,56,512]{2,1,0:T(8,128)(2,1)}), bf16[16,56,512]{2,1,0:T(8,128)(2,1)S(1)}, u32[]{:S(2)}, u32[]{:S(2)}) async-start(bf16[16,56,512]{2,1,0:T(8,128)(2,1)} %fusion.13), calls=%async_computation.2 | async-start | bytes 1835008 | tf_op jit(solution)/shard_map/all_to_all | solution.py:850
  359.2 1.3 collective-permute-start.21
  360.4 1.9 constant_dynamic-update-slice_fusion.24
  362.3 1.9 constant_dynamic-update-slice_fusion.23
  364.2 6.2 %fusion = f32[640,768]{1,0:T(8,128)} fusion(bf16[640,1920]{1,0:T(8,128)(2,1)} %constant_dynamic-update-slice_fusion.23, bf16[768,768]{1,0:T(8,128)(2,1)} %collective-permute-done.20, bf16[768,384]{1,0:T(8,128)(2,1)} %slice.362, bf16[768,768]{1,0:T(8,128)(2,1)} %bitcast.31), kind=kOutput, calls=%fused_computation.5 | convolution fusion | flops 1896284160 | bytes 7372800 | tf_op jit(solution)/shard_map/dot_general | solution.py:40
  372.9 2.7 add_add_fusion
  376.4 1.2 slice_bitcast_fusion
  377.6 6.6 %all-to-all-done.2 = bf16[16,56,512]{2,1,0:T(8,128)(2,1)S(1)} async-done(((bf16[16,56,512]{2,1,0:T(8,128)(2,1)}), bf16[16,56,512]{2,1,0:T(8,128)(2,1)S(1)}, u32[]{:S(2)}, u32[]{:S(2)}) %all-to-all-start.2) | async-done | bytes 917536 | tf_op jit(solution)/shard_map/all_to_all | solution.py:850
  384.4 1.5 collective-permute-start.23
  393.5 1.4 slice_convert_fusion.2
  (345 shorter events, 58.5 us)
Async XLA Ops:
  7.2 141.3 %all-gather.2.cloned.1.call-start = ((), (), s32[]{:S(2)}) async-start(), calls=%async_computation.4 | async-start | bytes 11489280 | tf_op jit(solution)/shard_map/all_gather | solution.py:743
  11.6 14.6 %collective-permute-start = (bf16[48,768]{1,0:T(8,128)(2,1)S(1)}, bf16[48,768]{1,0:T(8,128)(2,1)S(1)}, u32[]{:S(2)}, u32[]{:S(2)}) collective-permute-start(bf16[48,768]{1,0:T(8,128)(2,1)S(1)} %constant_dynamic-update-slice_fusion), channel_id=1, source_target_pairs={{0,8},{1,9},{2,10},{3,11},{4,12},{5,13},{6,14},{7,15},{8,0},{9,1},... | collective-permute-start | bytes 221192 | tf_op jit(solution)/shard_map/ppermute | solution.py:613
  17.1 8.6 %copy-start.41 = (bf16[192,768]{1,0:T(8,128)(2,1)S(1)}, bf16[192,768]{1,0:T(8,128)(2,1)}, u32[]{:S(2)}) copy-start(bf16[192,768]{1,0:T(8,128)(2,1)} %param.36) | copy-start | bytes 884740
  17.1 9.7 %collective-permute-start.1 = (bf16[48,896]{1,0:T(8,128)(2,1)S(1)}, bf16[48,896]{1,0:T(8,128)(2,1)S(1)}, u32[]{:S(2)}, u32[]{:S(2)}) collective-permute-start(bf16[48,896]{1,0:T(8,128)(2,1)S(1)} %constant_dynamic-update-slice_fusion.6), channel_id=1, source_target_pairs={{0,2},{1,3},{2,0},{3,1},{4,6},{5,7},{6,4},{7,5},{8,10},{9,11},{10,... | collective-permute-start | bytes 258056 | tf_op jit(solution)/shard_map/ppermute | solution.py:613
  19.9 6.1 %copy-start.52 = (bf16[2,48]{1,0:T(2,128)(2,1)S(1)}, bf16[2,48]{1,0:T(2,128)(2,1)}, u32[]{:S(2)}) copy-start(bf16[2,48]{1,0:T(2,128)(2,1)} %param.38) | copy-start | bytes 580
  19.9 6.2 %copy-start.53 = (bf16[2,48]{1,0:T(2,128)(2,1)S(1)}, bf16[2,48]{1,0:T(2,128)(2,1)}, u32[]{:S(2)}) copy-start(bf16[2,48]{1,0:T(2,128)(2,1)} %param.39) | copy-start | bytes 580
  19.9 6.3 %copy-start.50 = (bf16[48]{0:T(256)(128)(2,1)S(1)}, bf16[48]{0:T(256)(128)(2,1)}, u32[]{:S(2)}) copy-start(bf16[48]{0:T(256)(128)(2,1)} %param.37) | copy-start | bytes 292
  19.9 6.3 %copy-start.51 = (bf16[192]{0:T(256)(128)(2,1)S(1)}, bf16[192]{0:T(256)(128)(2,1)}, u32[]{:S(2)}) copy-start(bf16[192]{0:T(256)(128)(2,1)} %param.35) | copy-start | bytes 1156
  19.9 12.1 %collective-permute-start.2 = (bf16[256,768]{1,0:T(8,128)(2,1)S(1)}, bf16[256,768]{1,0:T(8,128)(2,1)S(1)}, u32[]{:S(2)}, u32[]{:S(2)}) collective-permute-start(bf16[256,768]{1,0:T(8,128)(2,1)S(1)} %get-tuple-element.139), channel_id=1, source_target_pairs={{0,16},{16,0},{1,17},{17,1},{2,18},{18,2},{3,19},{19,3},{4,20},{20... | collective-permute-start | bytes 1179656 | tf_op jit(solution)/shard_map/ppermute | solution.py:604
  21.5 19.1 %collective-permute-start.5 = (bf16[256,768]{1,0:T(8,128)(2,1)S(1)}, bf16[256,768]{1,0:T(8,128)(2,1)}, u32[]{:S(2)}, u32[]{:S(2)}) collective-permute-start(bf16[256,768]{1,0:T(8,128)(2,1)S(1)} %get-tuple-element.138), channel_id=1, source_target_pairs={{0,16},{16,0},{1,17},{17,1},{2,18},{18,2},{3,19},{19,3},{4,20},{20... | collective-permute-start | bytes 1179656 | tf_op jit(solution)/shard_map/ppermute | solution.py:604
  22.0 24.9 %collective-permute-start.8 = (bf16[192,768]{1,0:T(8,128)(2,1)}, bf16[192,768]{1,0:T(8,128)(2,1)}, u32[]{:S(2)}, u32[]{:S(2)}) collective-permute-start(bf16[192,768]{1,0:T(8,128)(2,1)} %bitcast.184), channel_id=1, source_target_pairs={{0,16},{16,0},{1,17},{17,1},{2,18},{18,2},{3,19},{19,3},{4,20},{20... | collective-permute-start | bytes 884744 | tf_op jit(solution)/shard_map/ppermute | solution.py:604
  23.5 8.5 %copy-start.47 = (s32[512]{0:T(512)}, s32[512]{0:T(512)S(1)}, u32[]{:S(2)}) copy-start(s32[512]{0:T(512)S(1)} %fusion.37) | copy-start | bytes 6148
  26.2 25.6 %collective-permute-start.11 = (bf16[128,768]{1,0:T(8,128)(2,1)}, bf16[128,768]{1,0:T(8,128)(2,1)}, u32[]{:S(2)}, u32[]{:S(2)}) collective-permute-start(bf16[128,768]{1,0:T(8,128)(2,1)} %bitcast.29.query_ref), channel_id=1, source_target_pairs={{0,16},{16,0},{1,17},{17,1},{2,18},{18,2},{3,19},{19,3},{4,20},{20... | collective-permute-start | bytes 589832 | tf_op jit(solution)/shard_map/ppermute | solution.py:604
  32.0 10.9 %copy-start.39 = (bf16[256,768]{1,0:T(8,128)(2,1)}, bf16[256,768]{1,0:T(8,128)(2,1)S(1)}, u32[]{:S(2)}) copy-start(bf16[256,768]{1,0:T(8,128)(2,1)S(1)} %collective-permute-done.2) | copy-start | bytes 1179652
  32.1 8.5 %collective-permute-start.4 = (bf16[2,48,896]{2,1,0:T(8,128)(2,1)S(1)}, bf16[2,48,896]{2,1,0:T(8,128)(2,1)S(1)}, u32[]{:S(2)}, u32[]{:S(2)}) collective-permute-start(bf16[2,48,896]{2,1,0:T(8,128)(2,1)S(1)} %maximum_select_fusion.13), channel_id=1, source_target_pairs={{0,8},{1,9},{2,10},{3,11},{4,12},{5,13},{6,14},{7,15},{8,0},{9,1},... | collective-permute-start | bytes 516104 | tf_op jit(solution)/shard_map/ppermute | solution.py:613
  32.5 8.1 %collective-permute-start.3 = (bf16[2,48,768]{2,1,0:T(8,128)(2,1)S(1)}, bf16[2,48,768]{2,1,0:T(8,128)(2,1)S(1)}, u32[]{:S(2)}, u32[]{:S(2)}) collective-permute-start(bf16[2,48,768]{2,1,0:T(8,128)(2,1)S(1)} %maximum_select_fusion.16), channel_id=1, source_target_pairs={{0,4},{1,5},{2,6},{3,7},{4,0},{5,1},{6,2},{7,3},{8,12},{9,13},{10,... | collective-permute-start | bytes 442376 | tf_op jit(solution)/shard_map/ppermute | solution.py:613
  40.6 8.5 %collective-permute-start.7 = (bf16[2,2,48,896]{3,2,1,0:T(8,128)(2,1)S(1)}, bf16[2,2,48,896]{3,2,1,0:T(8,128)(2,1)S(1)}, u32[]{:S(2)}, u32[]{:S(2)}) collective-permute-start(bf16[2,2,48,896]{3,2,1,0:T(8,128)(2,1)S(1)} %maximum_select_fusion.7), channel_id=1, source_target_pairs={{0,4},{1,5},{2,6},{3,7},{4,0},{5,1},{6,2},{7,3},{8,12},{9,13},{10,... | collective-permute-start | bytes 1032200 | tf_op jit(solution)/shard_map/ppermute | solution.py:613
  42.3 6.8 %collective-permute-start.6 = (bf16[2,2,48,768]{3,2,1,0:T(8,128)(2,1)S(1)}, bf16[2,2,48,768]{3,2,1,0:T(8,128)(2,1)S(1)}, u32[]{:S(2)}, u32[]{:S(2)}) collective-permute-start(bf16[2,2,48,768]{3,2,1,0:T(8,128)(2,1)S(1)} %maximum_select_fusion.9), channel_id=1, source_target_pairs={{0,2},{1,3},{2,0},{3,1},{4,6},{5,7},{6,4},{7,5},{8,10},{9,11},{10,... | collective-permute-start | bytes 884744 | tf_op jit(solution)/shard_map/ppermute | solution.py:613
  43.1 7.6 %copy-start.43 = (bf16[48,768]{1,0:T(8,128)(2,1)S(1)}, bf16[48,768]{1,0:T(8,128)(2,1)}, u32[]{:S(2)}) copy-start(bf16[48,768]{1,0:T(8,128)(2,1)} %param.30) | copy-start | bytes 221188
  49.3 3.4 collective-permute-start.10
  50.2 2.5 collective-permute-start.9
  51.8 5.0 %copy-start.44 = (s32[1,1408]{1,0:T(1,128)S(1)}, s32[1,1408]{1,0:T(1,128)}, u32[]{:S(2)}) copy-start(s32[1,1408]{1,0:T(1,128)} %param.24) | copy-start | bytes 16900
  51.8 5.0 %copy-start.49 = (s32[1,384]{1,0:T(1,128)S(1)}, s32[1,384]{1,0:T(1,128)}, u32[]{:S(2)}) copy-start(s32[1,384]{1,0:T(1,128)} %param.26) | copy-start | bytes 4612
  51.8 5.1 %slice-start.2 = ((s32[1,1408]{1,0:T(1,128)}), s32[1,1024]{1,0:T(1,128)S(1)}, s32[]{:S(2)}) async-start(s32[1,1408]{1,0:T(1,128)} %param.24), calls=%async_computation.8 | async-start | bytes 8192 | tf_op jit(solution)/shard_map/slice | solution.py:775
  52.7 8.0 %copy-start.27 = (bf16[2,2,2,48,896]{4,3,2,1,0:T(8,128)(2,1)}, bf16[2,2,2,48,896]{4,3,2,1,0:T(8,128)(2,1)S(1)}, u32[]{:S(2)}) copy-start(bf16[2,2,2,48,896]{4,3,2,1,0:T(8,128)(2,1)S(1)} %collective-permute-done.10) | copy-start | bytes 2064388
  55.4 334.8 %reduce-scatter.2.cloned.1.call-start = ((), (), s32[]{:S(2)}) async-start(), calls=%async_computation.5 | async-start | bytes 10948608 | tf_op jit(solution)/shard_map/reduce_scatter | solution.py:817
  65.5 49.5 %copy-start.35 = (bf16[256,768]{1,0:T(8,128)(2,1)}, bf16[256,768]{1,0:T(8,128)(2,1)S(1)}, u32[]{:S(2)}) copy-start(bf16[256,768]{1,0:T(8,128)(2,1)S(1)} %maximum_select_fusion.6) | copy-start | bytes 1179652
  67.0 47.9 %copy-start.30 = (bf16[384,768]{1,0:T(8,128)(2,1)}, bf16[384,768]{1,0:T(8,128)(2,1)S(1)}, u32[]{:S(2)}) copy-start(bf16[384,768]{1,0:T(8,128)(2,1)S(1)} %maximum_select_fusion.5) | copy-start | bytes 1769476
  69.0 45.9 %copy-start.23 = (bf16[1024,768]{1,0:T(8,128)(2,1)}, bf16[1024,768]{1,0:T(8,128)(2,1)S(1)}, u32[]{:S(2)}) copy-start(bf16[1024,768]{1,0:T(8,128)(2,1)S(1)} %maximum_select_fusion) | copy-start | bytes 4718596
  71.2 45.2 %copy-start.3 = (bf16[2432,384]{1,0:T(8,128)(2,1)}, bf16[2432,384]{1,0:T(8,128)(2,1)S(1)}, u32[]{:S(2)}) copy-start(bf16[2432,384]{1,0:T(8,128)(2,1)S(1)} %convolution_convert_fusion.rel_ref) | copy-start | bytes 5603332
  75.4 20.8 %copy-start.7 = (bf16[1664,768]{1,0:T(8,128)(2,1)}, bf16[1664,768]{1,0:T(8,128)(2,1)S(1)}, u32[]{:S(2)}) copy-start(bf16[1664,768]{1,0:T(8,128)(2,1)S(1)} %convolution_convert_fusion.1.q_ref.k_ref.v_ref) | copy-start | bytes 7667716
  94.7 43.4 %collective-permute-start.12 = (bf16[640,128]{1,0:T(8,128)(2,1)S(1)}, bf16[640,128]{1,0:T(8,128)(2,1)S(1)}, u32[]{:S(2)}, u32[]{:S(2)}) collective-permute-start(bf16[640,128]{1,0:T(8,128)(2,1)S(1)} %pad_maximum_fusion.18), channel_id=1, source_target_pairs={{0,16},{16,0},{1,17},{17,1},{2,18},{18,2},{3,19},{19,3},{4,20},{20... | collective-permute-start | bytes 491528 | tf_op jit(solution)/shard_map/ppermute | solution.py:604
  116.5 18.6 %copy-start.1 = (bf16[1664,384]{1,0:T(8,128)(2,1)}, bf16[1664,384]{1,0:T(8,128)(2,1)S(1)}, u32[]{:S(2)}) copy-start(bf16[1664,384]{1,0:T(8,128)(2,1)S(1)} %convolution_convert_fusion.2.q_ref.k_ref.v_ref) | copy-start | bytes 3833860
  135.1 10.1 %copy-start.13 = (f32[1280,128]{1,0:T(8,128)}, f32[1280,128]{1,0:T(8,128)S(1)}, u32[]{:S(2)}) copy-start(f32[1280,128]{1,0:T(8,128)S(1)} %get-tuple-element.106.inv_ref) | copy-start | bytes 1966084
  135.1 7.1 %collective-permute-start.13 = (bf16[640,128]{1,0:T(8,128)(2,1)S(1)}, bf16[640,128]{1,0:T(8,128)(2,1)S(1)}, u32[]{:S(2)}, u32[]{:S(2)}) collective-permute-start(bf16[640,128]{1,0:T(8,128)(2,1)S(1)} %pad_maximum_fusion.19), channel_id=1, source_target_pairs={{0,16},{16,0},{1,17},{17,1},{2,18},{18,2},{3,19},{19,3},{4,20},{20... | collective-permute-start | bytes 491528 | tf_op jit(solution)/shard_map/ppermute | solution.py:604
  136.7 8.3 %collective-permute-start.14 = (bf16[640,128]{1,0:T(8,128)(2,1)S(1)}, bf16[640,128]{1,0:T(8,128)(2,1)S(1)}, u32[]{:S(2)}, u32[]{:S(2)}) collective-permute-start(bf16[640,128]{1,0:T(8,128)(2,1)S(1)} %pad_maximum_fusion.20), channel_id=1, source_target_pairs={{0,16},{16,0},{1,17},{17,1},{2,18},{18,2},{3,19},{19,3},{4,20},{20... | collective-permute-start | bytes 491528 | tf_op jit(solution)/shard_map/ppermute | solution.py:604
  146.5 217.8 %collective-permute-start.20 = (bf16[768,768]{1,0:T(8,128)(2,1)}, bf16[768,768]{1,0:T(8,128)(2,1)}, u32[]{:S(2)}, u32[]{:S(2)}) collective-permute-start(bf16[768,768]{1,0:T(8,128)(2,1)} %bitcast.31), channel_id=1, source_target_pairs={{0,16},{16,0},{1,17},{17,1},{2,18},{18,2},{3,19},{19,3},{4,20},{20... | collective-permute-start | bytes 3538952 | tf_op jit(solution)/shard_map/ppermute | solution.py:604
  146.9 226.0 %collective-permute-start.22 = (bf16[768,384]{1,0:T(8,128)(2,1)}, bf16[768,384]{1,0:T(8,128)(2,1)}, u32[]{:S(2)}, u32[]{:S(2)}) collective-permute-start(bf16[768,384]{1,0:T(8,128)(2,1)} %slice.362), channel_id=1, source_target_pairs={{0,16},{16,0},{1,17},{17,1},{2,18},{18,2},{3,19},{19,3},{4,20},{20... | collective-permute-start | bytes 1769480 | tf_op jit(solution)/shard_map/ppermute | solution.py:604
  192.9 5.2 %copy-start.45 = (f32[1,3072]{1,0:T(1,128)S(1)}, f32[1,3072]{1,0:T(1,128)}, u32[]{:S(2)}) copy-start(f32[1,3072]{1,0:T(1,128)} %get-tuple-element.97) | copy-start | bytes 36868
  192.9 5.6 %copy-start.46 = (f32[8,768]{1,0:T(8,128)S(1)}, f32[8,768]{1,0:T(8,128)}, u32[]{:S(2)}) copy-start(f32[8,768]{1,0:T(8,128)} %get-tuple-element.98) | copy-start | bytes 73732
  197.6 7.5 %collective-permute-start.15 = (bf16[640,128]{1,0:T(8,128)(2,1)}, bf16[640,128]{1,0:T(8,128)(2,1)}, u32[]{:S(2)}, u32[]{:S(2)}) collective-permute-start(bf16[640,128]{1,0:T(8,128)(2,1)} %get-tuple-element.133), channel_id=1, source_target_pairs={{0,16},{16,0},{1,17},{17,1},{2,18},{18,2},{3,19},{19,3},{4,20},{20... | collective-permute-start | bytes 491528 | tf_op jit(solution)/shard_map/ppermute | solution.py:604
  198.8 51.5 %collective-permute-start.16 = (bf16[640,128]{1,0:T(8,128)(2,1)}, bf16[640,128]{1,0:T(8,128)(2,1)}, u32[]{:S(2)}, u32[]{:S(2)}) collective-permute-start(bf16[640,128]{1,0:T(8,128)(2,1)} %get-tuple-element.136), channel_id=1, source_target_pairs={{0,16},{16,0},{1,17},{17,1},{2,18},{18,2},{3,19},{19,3},{4,20},{20... | collective-permute-start | bytes 491528 | tf_op jit(solution)/shard_map/ppermute | solution.py:604
  200.4 93.3 %collective-permute-start.17 = (bf16[640,128]{1,0:T(8,128)(2,1)}, bf16[640,128]{1,0:T(8,128)(2,1)}, u32[]{:S(2)}, u32[]{:S(2)}) collective-permute-start(bf16[640,128]{1,0:T(8,128)(2,1)} %get-tuple-element.134), channel_id=1, source_target_pairs={{0,16},{16,0},{1,17},{17,1},{2,18},{18,2},{3,19},{19,3},{4,20},{20... | collective-permute-start | bytes 491528 | tf_op jit(solution)/shard_map/ppermute | solution.py:604
  200.9 6.0 %copy-start.4 = (bf16[2432,384]{1,0:T(8,128)(2,1)S(1)}, bf16[2432,384]{1,0:T(8,128)(2,1)}, u32[]{:S(2)}) copy-start(bf16[2432,384]{1,0:T(8,128)(2,1)} %copy-done.3) | copy-start | bytes 5603332
  209.9 29.8 %copy-start.24 = (bf16[1024,768]{1,0:T(8,128)(2,1)S(1)}, bf16[1024,768]{1,0:T(8,128)(2,1)}, u32[]{:S(2)}) copy-start(bf16[1024,768]{1,0:T(8,128)(2,1)} %copy-done.23) | copy-start | bytes 4718596
  209.9 29.8 %copy-start.31 = (bf16[384,768]{1,0:T(8,128)(2,1)S(1)}, bf16[384,768]{1,0:T(8,128)(2,1)}, u32[]{:S(2)}) copy-start(bf16[384,768]{1,0:T(8,128)(2,1)} %copy-done.30) | copy-start | bytes 1769476
  209.9 29.8 %copy-start.36 = (bf16[256,768]{1,0:T(8,128)(2,1)S(1)}, bf16[256,768]{1,0:T(8,128)(2,1)}, u32[]{:S(2)}) copy-start(bf16[256,768]{1,0:T(8,128)(2,1)} %copy-done.35) | copy-start | bytes 1179652
  245.6 52.4 %all-to-all-start = ((bf16[16,56,512]{2,1,0:T(8,128)(2,1)}), bf16[16,56,512]{2,1,0:T(8,128)(2,1)}, u32[]{:S(2)}, u32[]{:S(2)}) async-start(bf16[16,56,512]{2,1,0:T(8,128)(2,1)} %fusion.12), calls=%async_computation | async-start | bytes 1835008 | tf_op jit(solution)/shard_map/all_to_all | solution.py:850
  290.7 4.9 %copy-start.22 = (bf16[38,64,384]{2,1,0:T(8,128)(2,1)S(1)}, bf16[38,64,384]{2,1,0:T(8,128)(2,1)}, u32[]{:S(2)}) copy-start(bf16[38,64,384]{2,1,0:T(8,128)(2,1)} %get-tuple-element.161) | copy-start | bytes 5603332
  290.8 71.5 %collective-permute-start.19 = (bf16[640,384]{1,0:T(8,128)(2,1)}, bf16[640,384]{1,0:T(8,128)(2,1)}, u32[]{:S(2)}, u32[]{:S(2)}) collective-permute-start(bf16[640,384]{1,0:T(8,128)(2,1)} %pad_maximum_fusion.10), channel_id=1, source_target_pairs={{0,16},{16,0},{1,17},{17,1},{2,18},{18,2},{3,19},{19,3},{4,20},{20... | collective-permute-start | bytes 1474568 | tf_op jit(solution)/shard_map/ppermute | solution.py:604
  292.7 66.5 %collective-permute-start.18 = (bf16[640,384]{1,0:T(8,128)(2,1)}, bf16[640,384]{1,0:T(8,128)(2,1)}, u32[]{:S(2)}, u32[]{:S(2)}) collective-permute-start(bf16[640,384]{1,0:T(8,128)(2,1)} %pad_maximum_fusion.9), channel_id=1, source_target_pairs={{0,16},{16,0},{1,17},{17,1},{2,18},{18,2},{3,19},{19,3},{4,20},{20... | collective-permute-start | bytes 1474568 | tf_op jit(solution)/shard_map/ppermute | solution.py:604
  298.0 8.5 %copy-start.14 = (f32[1280,128]{1,0:T(8,128)S(1)}, f32[1280,128]{1,0:T(8,128)}, u32[]{:S(2)}) copy-start(f32[1280,128]{1,0:T(8,128)} %copy-done.13) | copy-start | bytes 1966084
  300.1 44.3 %all-to-all-start.1 = ((bf16[16,48,512]{2,1,0:T(8,128)(2,1)}), bf16[16,48,512]{2,1,0:T(8,128)(2,1)}, u32[]{:S(2)}, u32[]{:S(2)}) async-start(bf16[16,48,512]{2,1,0:T(8,128)(2,1)} %pad_maximum_fusion.2), calls=%async_computation.1 | async-start | bytes 1572864 | tf_op jit(solution)/shard_map/all_to_all | solution.py:850
  341.0 6.8 %copy-start.33 = (bf16[384,768]{1,0:T(8,128)(2,1)S(1)}, bf16[384,768]{1,0:T(8,128)(2,1)}, u32[]{:S(2)}) copy-start(bf16[384,768]{1,0:T(8,128)(2,1)} %copy-done.30) | copy-start | bytes 1769476
  341.0 6.8 %copy-start.38 = (bf16[256,768]{1,0:T(8,128)(2,1)S(1)}, bf16[256,768]{1,0:T(8,128)(2,1)}, u32[]{:S(2)}) copy-start(bf16[256,768]{1,0:T(8,128)(2,1)} %copy-done.35) | copy-start | bytes 1179652
  347.1 23.4 %collective-permute-start.24 = (bf16[512]{0:T(512)(128)(2,1)S(1)}, bf16[512]{0:T(512)(128)(2,1)S(1)}, u32[]{:S(2)}, u32[]{:S(2)}) collective-permute-start(bf16[512]{0:T(512)(128)(2,1)S(1)} %fusion.41), channel_id=1, source_target_pairs={{0,16},{16,0},{1,17},{17,1},{2,18},{18,2},{3,19},{19,3},{4,20},{20... | collective-permute-start | bytes 3080 | tf_op jit(solution)/shard_map/ppermute | solution.py:604
  352.1 32.1 %all-to-all-start.2 = ((bf16[16,56,512]{2,1,0:T(8,128)(2,1)}), bf16[16,56,512]{2,1,0:T(8,128)(2,1)S(1)}, u32[]{:S(2)}, u32[]{:S(2)}) async-start(bf16[16,56,512]{2,1,0:T(8,128)(2,1)} %fusion.13), calls=%async_computation.2 | async-start | bytes 1835008 | tf_op jit(solution)/shard_map/all_to_all | solution.py:850
  359.2 13.8 %collective-permute-start.21 = (bf16[640,384]{1,0:T(8,128)(2,1)S(1)}, bf16[640,384]{1,0:T(8,128)(2,1)}, u32[]{:S(2)}, u32[]{:S(2)}) collective-permute-start(bf16[640,384]{1,0:T(8,128)(2,1)S(1)} %pad_maximum_fusion.11), channel_id=1, source_target_pairs={{0,16},{16,0},{1,17},{17,1},{2,18},{18,2},{3,19},{19,3},{4,20},{20... | collective-permute-start | bytes 1474568 | tf_op jit(solution)/shard_map/ppermute | solution.py:604
  364.2 6.2 %copy-start.34 = (f32[56,512]{1,0:T(8,128)S(1)}, f32[56,512]{1,0:T(8,128)}, u32[]{:S(2)}) copy-start(f32[56,512]{1,0:T(8,128)} %convert_reduce_fusion.1) | copy-start | bytes 344068
  364.2 8.7 %copy-start.16 = (f32[640,768]{1,0:T(8,128)S(1)}, f32[640,768]{1,0:T(8,128)}, u32[]{:S(2)}) copy-start(f32[640,768]{1,0:T(8,128)} %get-tuple-element.91) | copy-start | bytes 5898244
  376.4 8.0 %slice-start.1 = ((f32[48,512]{1,0:T(8,128)}), f32[48,384]{1,0:T(8,128)S(1)}, s32[]{:S(2)}) async-start(f32[48,512]{1,0:T(8,128)} %convert_reduce_fusion.2), calls=%async_computation.7 | async-start | bytes 147456 | tf_op jit(solution)/shard_map/slice | solution.py:893
  376.4 9.6 %slice-start = ((f32[48,512]{1,0:T(8,128)}), f32[48,128]{1,0:T(8,128)S(1)}, s32[]{:S(2)}) async-start(f32[48,512]{1,0:T(8,128)} %convert_reduce_fusion.2), calls=%async_computation.6 | async-start | bytes 49152 | tf_op jit(solution)/shard_map/slice | solution.py:918
  384.4 7.2 %copy-start.48 = (s32[512]{0:T(512)S(1)}, s32[512]{0:T(512)}, u32[]{:S(2)}) copy-start(s32[512]{0:T(512)} %copy-done.47) | copy-start | bytes 6148
  384.4 4.2 %collective-permute-start.23 = (bf16[24,1152]{1,0:T(8,128)(2,1)S(1)}, bf16[24,1152]{1,0:T(8,128)(2,1)S(1)}, u32[]{:S(2)}, u32[]{:S(2)}) collective-permute-start(bf16[24,1152]{1,0:T(8,128)(2,1)S(1)} %dynamic-slice_convert_fusion), channel_id=1, source_target_pairs={{0,16},{16,0},{1,17},{17,1},{2,18},{18,2},{3,19},{19,3},{4,20},{20... | collective-permute-start | bytes 165896 | tf_op jit(solution)/shard_map/ppermute | solution.py:604
  (23 other events, 51.4 us)
Sparse Core Ops, SparseCore 0:
  55.5 89.5 all-gather.1
  201.1 177.8 reduce-scatter.1
